TPU v7x, 32 devices: a whole 2x2x4 slice. The times are simulated.
32 devices in a mesh: req: 16 (over z, x, core), mdl: 2 (over y).
Axes of the slice: x: 2, y: 2, z: 4, core: 2. Of those that a mesh axis runs over, the one named last changes fastest.
Arguments:
- hidden: bfloat16 [4096, 1536], P(('req', 'mdl')), may hold values from -6 to 6
- input_gain: float32 [1536], replicated, may hold values from 0.1 to 1.9
- gate_proj: bfloat16 [1536, 3072], P('req', 'mdl'), may hold values from -0.15625 to 0.15625
- value_proj: bfloat16 [1536, 3072], P('req', 'mdl'), may hold values from -0.15625 to 0.15625
- state_proj: bfloat16 [1536, 256], P('req'), may hold values from -0.15625 to 0.15625
- step_proj: bfloat16 [1536, 48], P('req', 'mdl'), may hold values from -0.15625 to 0.15625
- conv_value: float32 [5, 3072], P(None, 'mdl'), may hold values from -3 to 3
- conv_state: float32 [5, 256], replicated, may hold values from -3 to 3
- step_bias: float32 [48], P('mdl'), may hold values from -4 to -1
- decay_log: float32 [48], P('mdl'), may hold values from -4 to 0
- skip_gain: float32 [48], P('mdl'), may hold values from 0.5 to 1.5
- output_gain: float32 [3072], P('mdl'), may hold values from 0.1 to 1.9
- out_proj: bfloat16 [3072, 1536], P('mdl', 'req'), may hold values from -0.109375 to 0.109375
- state_start: float32 [32, 48, 64, 128], P('req', 'mdl'), may hold values from -0.8 to 0.8
- edge_value: bfloat16 [32, 3, 3072], P('req', None, 'mdl'), may hold values from -6 to 6
- edge_state: bfloat16 [32, 3, 256], P('req'), may hold values from -6 to 6
- lengths: int32 [32], P('req'), may hold values from 1 to 128, as said below
- accepted: int32 [32], P('req'), may hold values from 1 to 128, as said below
Outputs:
- mixed: bfloat16 [4096, 1536], P(('req', 'mdl'))
- state_final: float32 [32, 48, 64, 128], P(('req', 'mdl'))
- edge_final: bfloat16 [32, 3, 3328], P(('req', 'mdl'))
Inputs may be any that keep to these rules, and one draw needn't show every extreme that they name: `lengths`: one request's draft fills all 128 slots. accepted[r] <= lengths[r]; the request whose draft fills all slots accepts all of it.
All inputs are finite; a program needn't handle non-finite values.
Results may differ from a plain program's by a relative error of at most 0.009.
Values may be sent and summed in bfloat16 or wider, within the bound.
A program may use at most 64 MiB of HBM per device.

v0:
```python
import jax
import jax.numpy as jnp
from jax import lax
from jax.sharding import PartitionSpec as P

EPSILON = 1e-05
HIGHEST = lax.Precision.HIGHEST


def local(
    hidden,
    input_gain,
    gate_proj,
    value_proj,
    state_proj,
    step_proj,
    conv_value,
    conv_state,
    step_bias,
    decay_log,
    skip_gain,
    output_gain,
    out_proj,
    state_start,
    edge_value,
    edge_state,
    lengths,
    accepted,
):
    requests, heads_here, head_dim, nstate = state_start.shape
    rows_dev = hidden.shape[0]
    span = rows_dev * lax.axis_size("mdl") // requests
    here_count = rows_dev // span
    group_rows = requests * span
    inner_here = heads_here * head_dim
    width_k = conv_value.shape[0] - 1
    edge_count = width_k - 1
    my_index = lax.axis_index("mdl")
    floats = hidden.astype(jnp.float32)
    normed = (
        floats * lax.rsqrt(jnp.mean(floats * floats, -1, keepdims=True) + EPSILON) * input_gain
    ).astype(jnp.bfloat16)
    widths = (gate_proj.shape[1], value_proj.shape[1], state_proj.shape[1], step_proj.shape[1])
    first_end = widths[0]
    second_end = first_end + widths[1]
    third_end = second_end + widths[2]
    whole = lax.all_gather(normed, "mdl", axis=0, tiled=True)
    joined_piece = jnp.concatenate(
        (
            lax.all_gather(gate_proj, "req", axis=0, tiled=True),
            lax.all_gather(value_proj, "req", axis=0, tiled=True),
            lax.all_gather(state_proj, "req", axis=0, tiled=True),
            lax.all_gather(step_proj, "req", axis=0, tiled=True),
        ),
        1,
    )
    joined = jnp.dot(whole, joined_piece, preferred_element_type=jnp.float32)
    gates = joined[:, :first_end].astype(jnp.bfloat16)
    values = joined[:, first_end:second_end].astype(jnp.bfloat16)
    readers = joined[:, second_end:third_end].astype(jnp.bfloat16)
    step_raw = joined[:, third_end:].astype(jnp.bfloat16)
    current = jnp.concatenate([values, readers], 1).reshape(requests, span, -1)
    edges = jnp.concatenate([edge_value, edge_state], 2)
    extended = jnp.concatenate([edges, current], 1).astype(jnp.float32)
    taps = jnp.concatenate([conv_value, conv_state], 1)
    convolved = taps[width_k][None, None, :] + jnp.zeros(
        (requests, span, taps.shape[1]), jnp.float32
    )
    for shift in range(width_k):
        convolved = convolved + taps[shift][None, None, :] * extended[:, shift : shift + span]
    active = jax.nn.silu(convolved).astype(jnp.bfloat16)
    vals = active[..., :inner_here].reshape(requests, span, heads_here, head_dim)
    inputs_b = active[..., inner_here : inner_here + nstate]
    reads_c = active[..., inner_here + nstate :]
    vals_f = vals.astype(jnp.float32)
    steps = jax.nn.softplus(
        step_raw.astype(jnp.float32).reshape(requests, span, heads_here) + step_bias
    )
    logs = -steps * jnp.exp(decay_log)
    running = jnp.cumsum(logs, axis=1)
    intersection = jnp.einsum("gtn,gsn->gts", reads_c, inputs_b, preferred_element_type=jnp.float32)
    positions = jnp.arange(span, dtype=jnp.int32)
    lower = positions[:, None] >= positions[None, :]
    spread = jnp.where(
        lower[None, :, :, None], running[:, :, None, :] - running[:, None, :, :], -jnp.inf
    )
    kernel = intersection[..., None] * jnp.exp(spread) * steps[:, None, :, :]
    outputs = jnp.einsum("gtsh,gshp->gthp", kernel, vals_f, precision=HIGHEST)
    carried = jnp.einsum(
        "gtn,ghpn->gthp", reads_c.astype(jnp.float32), state_start, precision=HIGHEST
    )
    outputs = outputs + jnp.exp(running)[..., None] * carried + skip_gain[:, None] * vals_f
    product = outputs.reshape(group_rows, inner_here) * jax.nn.silu(gates.astype(jnp.float32))
    squares = jnp.sum(product * product, -1)
    gated = (product * output_gain).astype(jnp.bfloat16)
    total_squares = lax.psum(squares, "mdl")
    scale = lax.rsqrt(total_squares / (inner_here * lax.axis_size("mdl")) + EPSILON)
    partial_terms = jnp.dot(
        gated,
        lax.all_gather(out_proj, "req", axis=1, tiled=True),
        preferred_element_type=jnp.float32,
    )
    mine = lax.psum_scatter(
        partial_terms.astype(jnp.bfloat16), "mdl", scatter_dimension=0, tiled=True
    ).astype(jnp.float32)
    my_scale = lax.dynamic_slice_in_dim(scale, my_index * rows_dev, rows_dev, 0)
    my_lengths = lax.dynamic_slice_in_dim(lengths, my_index * here_count, here_count, 0)
    live = (positions[None, :] < my_lengths[:, None]).reshape(rows_dev).astype(jnp.float32)
    mixed = (mine * my_scale[:, None] * live[:, None]).astype(jnp.bfloat16)
    last = accepted - 1
    chosen = (positions[None, :] == last[:, None]).astype(jnp.float32)
    running_last = jnp.sum(chosen[:, :, None] * running, axis=1)
    before = positions[None, :] <= last[:, None]
    reach = jnp.where(before[:, :, None], running_last[:, None, :] - running, -jnp.inf)
    weights_s = jnp.exp(reach) * steps
    gathered_state = jnp.einsum(
        "gsh,gshp,gsn->ghpn", weights_s, vals_f, inputs_b.astype(jnp.float32), precision=HIGHEST
    )
    state_here = jnp.exp(running_last)[:, :, None, None] * state_start + gathered_state
    picks = accepted[:, None] + jnp.arange(edge_count, dtype=jnp.int32)[None, :]
    selected = jnp.take_along_axis(extended, picks[:, :, None], axis=1)
    value_edges = selected[..., :inner_here].reshape(requests, edge_count, heads_here, head_dim)
    value_edges = value_edges.transpose(0, 2, 1, 3).reshape(
        requests, heads_here, edge_count * head_dim
    )
    states_home, edges_home = (
        lax.all_to_all(
            state_here.reshape(requests, heads_here, head_dim * nstate).astype(jnp.bfloat16),
            "mdl",
            split_axis=0,
            concat_axis=1,
            tiled=True,
        ).astype(jnp.float32),
        lax.all_to_all(
            value_edges.astype(jnp.bfloat16), "mdl", split_axis=0, concat_axis=1, tiled=True
        ).astype(value_edges.dtype),
    )
    heads_all = states_home.shape[1]
    state_final = states_home.reshape(here_count, heads_all, head_dim, nstate)
    edges_home = edges_home.reshape(here_count, heads_all, edge_count, head_dim).transpose(
        0, 2, 1, 3
    )
    edges_home = edges_home.reshape(here_count, edge_count, heads_all * head_dim)
    state_edges = lax.dynamic_slice_in_dim(
        selected[..., inner_here:], my_index * here_count, here_count, 0
    )
    edge_final = jnp.concatenate([edges_home, state_edges], 2).astype(jnp.bfloat16)
    return (mixed, state_final, edge_final)


def solution(mesh):
    return jax.shard_map(
        local,
        mesh=mesh,
        in_specs=(
            P(("req", "mdl"), None),
            P(),
            P("req", "mdl"),
            P("req", "mdl"),
            P("req", None),
            P("req", "mdl"),
            P(None, "mdl"),
            P(),
            P("mdl"),
            P("mdl"),
            P("mdl"),
            P("mdl"),
            P("mdl", "req"),
            P("req", "mdl", None, None),
            P("req", None, "mdl"),
            P("req", None, None),
            P("req"),
            P("req"),
        ),
        out_specs=(
            P(("req", "mdl"), None),
            P(("req", "mdl"), None, None, None),
            P(("req", "mdl"), None, None),
        ),
        check_vma=False,
    )
```

profile of v0, /device:TPU:0, one launch (start us, length us, event | category | flops | bytes accessed | tf_op | source)
XLA Modules:
  0.0 223.7 jit_solution(16343894568138646009)
XLA Ops:
  7.2 0.0 all-gather.5.cloned.1.call-start
  7.2 0.7 all-gather.5.cloned.1.call-update
  7.9 0.0 all-gather.7.cloned.1.call-start
  8.0 0.7 all-gather.7.cloned.1.call-update
  8.7 0.0 all-gather.9.cloned.1.call-start
  8.7 0.7 all-gather.9.cloned.1.call-update
  9.4 0.0 reduce-scatter.2.cloned.1.call-start
  9.5 23.7 %all-gather = bf16[16,96,24]{1,2,0:T(8,128)(2,1)S(1)} all-gather(bf16[1,96,24]{1,2,0:T(8,128)(2,1)} %bitcast.67), channel_id=1, replica_groups=mesh['req'=16,'mdl'=2] {'req'}, dimensions={0}, use_global_device_ids=true | all-gather | bytes 78336 | tf_op jit(solution)/shard_map/all_gather | solution.py:53
  33.2 0.2 copy.135
  33.4 0.7 copy.116
  34.1 0.7 copy.117
  34.8 0.7 exp.41
  35.5 0.7 fusion.50
  36.2 0.1 reshape.274
  36.3 1.2 dynamic_slice.10
  37.5 0.6 compare_convert_fusion.1
  38.2 0.8 constant_dynamic-update-slice_fusion.1
  39.0 0.7 constant_dynamic-update-slice_fusion
  39.7 0.1 slice_reduce_fusion.4
  39.8 0.2 fusion.35
  40.0 0.2 fusion.37
  40.2 12.0 %all_gather.18 = bf16[256,1536]{1,0:T(8,128)(2,1)S(1)} all-gather(bf16[128,1536]{1,0:T(8,128)(2,1)S(1)} %fusion.37), channel_id=1, replica_groups=mesh['req'=16,'mdl'=2] {'mdl'}, dimensions={0}, use_global_device_ids=true | all-gather | bytes 1179648 | tf_op jit(solution)/shard_map/all_gather | solution.py:47
  52.2 0.1 compare_and_fusion
  52.3 0.1 iota_compare_fusion.1
  52.4 21.1 %all_gather.21 = bf16[1536,256]{1,0:T(8,128)(2,1)S(1)} all-gather(bf16[96,256]{1,0:T(8,128)(2,1)S(1)} %copy-done.4), channel_id=1, replica_groups=mesh['req'=16,'mdl'=2] {'req'}, dimensions={0}, use_global_device_ids=true | all-gather | bytes 835584 | tf_op jit(solution)/shard_map/all_gather | solution.py:52
  73.5 51.8 %all-gather.7.cloned.1.call-done = bf16[1536,1536]{1,0:T(8,128)(2,1)} async-done(((bf16[96,1536]{1,0:T(8,128)(2,1)}), bf16[1536,1536]{1,0:T(8,128)(2,1)}) %all-gather.7.cloned.1.call-update) | async-done | bytes 4718608 | tf_op jit(solution)/shard_map/all_gather | solution.py:51
  125.3 9.4 %fusion.8 = bf16[256,3352]{0,1:T(8,128)(2,1)} fusion(bf16[256,1536]{1,0:T(8,128)(2,1)S(1)} %all_gather.18, bf16[1536,24]{1,0:T(8,128)(2,1)S(1)} %bitcast.64, bf16[1536,256]{1,0:T(8,128)(2,1)S(1)} %all_gather.21, bf16[1536,1536]{1,0:T(8,128)(2,1)} %all-gather.7.cloned.1.call-done, bf16[1536,1536]{1,0:T(8,128)(2,1)} %all-gather.5.cloned.1.call-done), kind=kOutput, calls=%fused_computation.9 | convolution fusion | flops 2678167552 | bytes 12800000 | tf_op jit(solution)/shard_map/dot_general | solution.py:57
  134.8 1.2 slice.82
  136.0 0.6 copy.136
  136.6 0.2 maximum_convert_fusion
  136.8 1.0 copy.129
  137.8 0.6 gather_fusion
  138.5 0.1 broadcast_select_fusion
  138.6 1.2 multiply_convert_fusion
  139.8 1.1 slice.90
  140.8 2.4 %copy.121 = bf16[2,128,1536]{1,2,0:T(8,128)(2,1)} copy(bf16[2,128,1536]{2,1,0:T(8,128)(2,1)} %slice.90) | data formatting | bytes 1572864 | tf_op jit(solution)/shard_map/slice | solution.py:72
  143.3 0.8 negate_multiply_fusion
  144.1 0.1 copy.123
  144.2 0.2 reduce_window_sum.11
  144.4 0.1 copy.124
  144.4 0.1 multiply_reduce_fusion.1
  144.6 0.1 copy.126
  144.6 0.2 fusion.44
  144.8 0.8 fusion.41
  145.7 5.0 %fusion.21 = f32[2,128,24,64]{1,3,2,0:T(8,128)S(1)} fusion(bf16[2,128,24,64]{1,3,2,0:T(8,128)(2,1)} %bitcast.60, f32[2,128,24,64]{1,3,2,0:T(8,128)S(1)} %fusion.41, f32[2,128,24]{1,2,0:T(8,128)S(1)} %get-tuple-element.9, f32[2,128,24]{1,2,0:T(8,128)S(1)} %copy.124, f32[2,128,128]{2,1,0:T(8,128)S(1)} %fusion.44, pred[128,128]{1,0:T(8,128)(4,1)S(1)} %iota_compare_fusion, ...), kind=kOutput, calls=%fused_computation.30 | convolution fusion | flops 609091584 | bytes 4153440 | tf_op jit(solution)/shard_map/gtsh,gshp->gthp/dot_general | solution.py:88
  150.7 1.2 copy.127
  151.9 27.7 %all-gather.9.cloned.1.call-done = bf16[1536,1536]{0,1:T(8,128)(2,1)} async-done(((bf16[1536,96]{0,1:T(8,128)(2,1)}), bf16[1536,1536]{0,1:T(8,128)(2,1)}) %all-gather.9.cloned.1.call-update) | async-done | bytes 4718608 | tf_op jit(solution)/shard_map/all_gather | solution.py:100
  179.6 5.3 %convolution_convert_fusion = bf16[256,1536]{1,0:T(8,128)(2,1)} fusion(bf16[1536,1536]{0,1:T(8,128)(2,1)} %all-gather.9.cloned.1.call-done, f32[1536]{0:T(1024)S(1)} %copy-done.7, f32[192,8,2,128]{3,2,1,0:T(2,128)S(1)} %bitcast.57, bf16[256,3352]{0,1:T(8,128)(2,1)} %fusion.8), kind=kOutput, calls=%fused_computation.16 | convolution fusion | flops 1211498496 | bytes 7870464 | tf_op jit(solution)/shard_map/dot_general | solution.py:98
  185.0 0.1 convert_element_type.120
  185.1 0.7 convert_element_type.122
  185.9 3.4 %all-to-all-start.1 = ((bf16[2,24,192]{2,1,0:T(8,128)(2,1)}), bf16[2,24,192]{2,1,0:T(8,128)(2,1)S(1)}, u32[]{:S(2)}, u32[]{:S(2)}) async-start(bf16[2,24,192]{2,1,0:T(8,128)(2,1)} %convert_element_type.122), calls=%async_computation.2 | async-start | bytes 49152 | tf_op jit(solution)/shard_map/all_to_all | solution.py:134
  189.3 1.7 multiply_reduce_fusion
  191.0 5.0 %psum.7 = f32[256]{0:T(256)S(1)} all-reduce(f32[256]{0:T(256)S(1)} %multiply_reduce_fusion), channel_id=1, replica_groups=mesh['req'=16,'mdl'=2] {'mdl'}, use_global_device_ids=true, to_apply=%region_4.5 | all-reduce | flops 256 | bytes 2048 | tf_op jit(solution)/shard_map/psum | solution.py:96
  196.0 0.1 exponential_multiply_fusion
  196.1 2.1 add_convert_fusion
  198.3 1.2 convert_element_type.117
  199.5 0.1 dynamic_slice.9
  199.6 3.5 %all-to-all-start = ((bf16[2,24,8192]{2,1,0:T(8,128)(2,1)}), bf16[2,24,8192]{2,1,0:T(8,128)(2,1)S(1)}, u32[]{:S(2)}, u32[]{:S(2)}) async-start(bf16[2,24,8192]{2,1,0:T(8,128)(2,1)} %convert_element_type.117), calls=%async_computation.1 | async-start | bytes 1572864 | tf_op jit(solution)/shard_map/all_to_all | solution.py:127
  203.1 0.1 convert_element_type.123
  203.2 0.1 concatenate.34
  203.3 0.6 pad_maximum_fusion
  203.9 9.9 %all-to-all-done = bf16[2,24,8192]{2,1,0:T(8,128)(2,1)S(1)} async-done(((bf16[2,24,8192]{2,1,0:T(8,128)(2,1)}), bf16[2,24,8192]{2,1,0:T(8,128)(2,1)S(1)}, u32[]{:S(2)}, u32[]{:S(2)}) %all-to-all-start) | async-done | bytes 786464 | tf_op jit(solution)/shard_map/all_to_all | solution.py:127
  213.9 1.3 copy.140
  215.2 2.0 multiply_convert_fusion.3
  (38 shorter events, 0.2 us)
Async XLA Ops:
  7.2 32.6 %copy-start.2 = (bf16[128,1536]{1,0:T(8,128)(2,1)S(1)}, bf16[128,1536]{1,0:T(8,128)(2,1)}, u32[]{:S(2)}) copy-start(bf16[128,1536]{1,0:T(8,128)(2,1)} %param.18) | copy-start | bytes 1179652
  7.2 32.8 %copy-start.5 = (f32[1536]{0:T(1024)S(1)}, f32[1536]{0:T(1024)}, u32[]{:S(2)}) copy-start(f32[1536]{0:T(1024)} %param.19) | copy-start | bytes 18436
  7.2 66.3 %all-gather.5.cloned.1.call-start = ((), (), s32[]{:S(2)}) async-start(), calls=%async_computation.3 | async-start | bytes 5013504 | tf_op jit(solution)/shard_map/all_gather | solution.py:50
  7.9 117.4 %all-gather.7.cloned.1.call-start = ((), (), s32[]{:S(2)}) async-start(), calls=%async_computation.4 | async-start | bytes 5013504 | tf_op jit(solution)/shard_map/all_gather | solution.py:51
  8.7 43.5 %copy-start.8 = (s32[2]{0:T(128)S(1)}, s32[2]{0:T(128)}, u32[]{:S(2)}) copy-start(s32[2]{0:T(128)} %param.35) | copy-start | bytes 28
  8.7 43.7 %copy-start.4 = (bf16[96,256]{1,0:T(8,128)(2,1)S(1)}, bf16[96,256]{1,0:T(8,128)(2,1)}, u32[]{:S(2)}) copy-start(bf16[96,256]{1,0:T(8,128)(2,1)} %param.22) | copy-start | bytes 147460
  8.7 170.9 %all-gather.9.cloned.1.call-start = ((), (), s32[]{:S(2)}) async-start(), calls=%async_computation.5 | async-start | bytes 5013504 | tf_op jit(solution)/shard_map/all_gather | solution.py:100
  9.4 205.8 %reduce-scatter.2.cloned.1.call-start = ((), (), s32[]{:S(2)}) async-start(), calls=%async_computation.6 | async-start | bytes 1179648 | tf_op jit(solution)/shard_map/reduce_scatter | solution.py:103
  138.6 1.2 copy-start.3
  139.8 5.0 %copy-start.1 = (bf16[2,128,1792]{2,1,0:T(8,128)(2,1)}, bf16[2,128,1792]{2,1,0:T(8,128)(2,1)S(1)}, u32[]{:S(2)}) copy-start(bf16[2,128,1792]{2,1,0:T(8,128)(2,1)S(1)} %multiply_convert_fusion) | copy-start | bytes 2752516
  139.8 3.5 %copy-start.6 = (f32[24]{0:T(128)S(1)}, f32[24]{0:T(128)}, u32[]{:S(2)}) copy-start(f32[24]{0:T(128)} %param.26) | copy-start | bytes 292
  140.8 4.0 %copy-start = (f32[2,24,64,128]{3,2,1,0:T(8,128)S(1)}, f32[2,24,64,128]{3,2,1,0:T(8,128)}, u32[]{:S(2)}) copy-start(f32[2,24,64,128]{3,2,1,0:T(8,128)} %param.31) | copy-start | bytes 4718596
  144.5 1.1 copy-start.9
  150.7 28.9 %copy-start.7 = (f32[1536]{0:T(1024)S(1)}, f32[1536]{0:T(1024)}, u32[]{:S(2)}) copy-start(f32[1536]{0:T(1024)} %param.29) | copy-start | bytes 18436
  179.6 5.4 %slice-start.1 = ((bf16[2,3,1792]{2,1,0:T(4,128)(2,1)}), bf16[2,3,1536]{2,1,0:T(4,128)(2,1)S(1)}, s32[]{:S(2)}) async-start(bf16[2,3,1792]{2,1,0:T(4,128)(2,1)} %copy-done.3), calls=%async_computation.8 | async-start | bytes 49152 | tf_op jit(solution)/shard_map/slice | solution.py:122
  185.9 13.7 %all-to-all-start.1 = ((bf16[2,24,192]{2,1,0:T(8,128)(2,1)}), bf16[2,24,192]{2,1,0:T(8,128)(2,1)S(1)}, u32[]{:S(2)}, u32[]{:S(2)}) async-start(bf16[2,24,192]{2,1,0:T(8,128)(2,1)} %convert_element_type.122), calls=%async_computation.2 | async-start | bytes 49152 | tf_op jit(solution)/shard_map/all_to_all | solution.py:134
  191.0 7.2 %slice-start = ((bf16[2,3,1792]{2,1,0:T(4,128)(2,1)}), bf16[2,3,256]{2,1,0:T(4,128)(2,1)S(1)}, s32[]{:S(2)}) async-start(bf16[2,3,1792]{2,1,0:T(4,128)(2,1)} %copy-done.3), calls=%async_computation.7 | async-start | bytes 8192 | tf_op jit(solution)/shard_map/slice | solution.py:145
  199.6 14.3 %all-to-all-start = ((bf16[2,24,8192]{2,1,0:T(8,128)(2,1)}), bf16[2,24,8192]{2,1,0:T(8,128)(2,1)S(1)}, u32[]{:S(2)}, u32[]{:S(2)}) async-start(bf16[2,24,8192]{2,1,0:T(8,128)(2,1)} %convert_element_type.117), calls=%async_computation.1 | async-start | bytes 1572864 | tf_op jit(solution)/shard_map/all_to_all | solution.py:127
Sparse Core Ops, SparseCore 0:
  10.3 59.6 all-gather.4
  72.3 53.0 all-gather.6
  127.6 51.9 all-gather.8
  185.1 16.3 reduce-scatter.1
where the time goes:
time: 225 us; the launch traced here: 224 us
  waiting for transfers between devices  91.5 us (41%)
  blocking collectives  61.9 us (28%)
  matrix products  22.9 us (10%)
  local copies, waits for them, and re-layouts  17.4 us (8%)
  between operations  14.1 us (6%)
  other arithmetic  8.84 us (4%)
  starting transfers between devices  7.12 us (3%)
    all_gather x1, waiting for transfers between devices, local(): lax.all_gather(value_proj, 'req', axis=0, tiled=True)  51.8 us
    all_gather x1, waiting for transfers between devices, local(): lax.all_gather(out_proj, 'req', axis=1, tiled=True)  27.7 us
    all_gather x1, blocking collectives, local(): lax.all_gather(step_proj, 'req', axis=0, tiled=True)  23.7 us
    all_gather x1, blocking collectives, local(): lax.all_gather(state_proj, 'req', axis=0, tiled=True)  21.1 us
    all_gather x1, blocking collectives, local(): whole = lax.all_gather(normed, 'mdl', axis=0, tiled=True)  12 us
    all_to_all x1, waiting for transfers between devices, local(): lax.all_to_all(state_here.reshape(requests, heads_here, head_dim * nstate...  9.93 us
    dot_general x1, matrix products, local(): joined = jnp.dot(whole, joined_piece, preferred_element_type=jnp.float32)  9.43 us
    dot_general x1, matrix products, local(): jnp.dot(gated, lax.all_gather(out_proj, 'req', axis=1, tiled=True), prefe...  5.33 us
  transfers between devices with their start and end apart: 6, of which 3 were waited for; matrix products, arithmetic and copies ran while one was open for 19% of the time, Pallas kernels for 0%

commit v1 on v0

--- a/solution.py
+++ b/solution.py
@@ -45,15 +45,8 @@
     second_end = first_end + widths[1]
     third_end = second_end + widths[2]
     whole = lax.all_gather(normed, "mdl", axis=0, tiled=True)
-    joined_piece = jnp.concatenate(
-        (
-            lax.all_gather(gate_proj, "req", axis=0, tiled=True),
-            lax.all_gather(value_proj, "req", axis=0, tiled=True),
-            lax.all_gather(state_proj, "req", axis=0, tiled=True),
-            lax.all_gather(step_proj, "req", axis=0, tiled=True),
-        ),
-        1,
-    )
+    packed = jnp.concatenate((gate_proj, value_proj, state_proj, step_proj), 1)
+    joined_piece = lax.all_gather(packed, "req", axis=0, tiled=True)
     joined = jnp.dot(whole, joined_piece, preferred_element_type=jnp.float32)
     gates = joined[:, :first_end].astype(jnp.bfloat16)
     values = joined[:, first_end:second_end].astype(jnp.bfloat16)
@@ -77,7 +70,9 @@
         step_raw.astype(jnp.float32).reshape(requests, span, heads_here) + step_bias
     )
     logs = -steps * jnp.exp(decay_log)
-    running = jnp.cumsum(logs, axis=1)
+    sooner = jnp.arange(span, dtype=jnp.int32)
+    triangle = (sooner[:, None] >= sooner[None, :]).astype(jnp.float32)
+    running = jnp.einsum("ts,gsh->gth", triangle, logs, precision=HIGHEST)
     intersection = jnp.einsum("gtn,gsn->gts", reads_c, inputs_b, preferred_element_type=jnp.float32)
     positions = jnp.arange(span, dtype=jnp.int32)
     lower = positions[:, None] >= positions[None, :]

time: 225 us -> 202 us (0.90)
  blocking collectives: 61.9 us -> 17.7 us
  waiting for transfers between devices: 91.5 us -> 118 us
  local copies, waits for them, and re-layouts: 17.4 us -> 13.4 us
    all_gather x2 -> x0, blocking collectives: 44.8 us -> none  [the longest x1 23.7 us: local(): lax.all_gather(step_proj, 'req', axis=0, tiled=True)]
    all_gather x2 -> x1, waiting for transfers between devices: 51.8 us -> 76.5 us  [local(): joined_piece = lax.all_gather(packed, 'req', axis=0, tiled=True)]
    all_gather x1, waiting for transfers between devices: 27.7 us -> 30.4 us  [local(): lax.all_gather(out_proj, 'req', axis=1, tiled=True)]
    slice x2, local copies, waits for them, and re-layouts: 3.47 us -> 1.22 us  [local(): active[..., :inner_here].reshape(requests, span, heads_here, head_dim)]
  transfers between devices with their start and end apart: 6 -> 5, of which waited for: 3 -> 3; matrix products, arithmetic and copies ran while one was open for 19% -> 17% of each run, Pallas kernels for 0% -> 0%
where the time goes in v1:
time: 202 us
  waiting for transfers between devices  118 us (58%)
  matrix products  21.2 us (10%)
  blocking collectives  17.7 us (9%)
  between operations  14.2 us (7%)
  local copies, waits for them, and re-layouts  13.4 us (7%)
  other arithmetic  10.6 us (5%)
  starting transfers between devices  6.91 us (3%)
    all_gather x1, waiting for transfers between devices, local(): joined_piece = lax.all_gather(packed, 'req', axis=0, tiled=True)  76.5 us
    all_gather x1, waiting for transfers between devices, local(): lax.all_gather(out_proj, 'req', axis=1, tiled=True)  30.4 us
    all_gather x1, blocking collectives, local(): whole = lax.all_gather(normed, 'mdl', axis=0, tiled=True)  12.8 us
    all_to_all x1, waiting for transfers between devices, local(): lax.all_to_all(state_here.reshape(requests, heads_here, head_dim * nstate...  9.9 us
    dot_general x1, matrix products, local(): joined = jnp.dot(whole, joined_piece, preferred_element_type=jnp.float32)  8.28 us
    dot_general x1, matrix products, local(): jnp.dot(gated, lax.all_gather(out_proj, 'req', axis=1, tiled=True), prefe...  5.3 us
    psum x1, blocking collectives, local(): total_squares = lax.psum(squares, 'mdl')  4.99 us
  transfers between devices with their start and end apart: 5, of which 3 were waited for; matrix products, arithmetic and copies ran while one was open for 17% of the time, Pallas kernels for 0%

profile of v1, /device:TPU:0, one launch (start us, length us, event | category | flops | bytes accessed | tf_op | source)
XLA Modules:
  0.0 201.5 jit_solution(17263862476050745246)
XLA Ops:
  7.2 0.0 copy-start.6
  7.2 0.0 copy-start.9
  7.2 0.0 copy-start.12
  7.2 0.0 copy-start.14
  7.3 0.0 all-gather.3.cloned.1.call-start
  7.3 0.9 copy.52
  8.2 2.0 pad_maximum_fusion
  10.1 0.0 all-gather.3.cloned.1.call-update
  10.2 0.0 all-gather.5.cloned.1.call-start
  10.2 0.7 all-gather.5.cloned.1.call-update
  10.9 0.0 reduce-scatter.2.cloned.1.call-start
  11.1 0.1 fusion.43
  11.1 0.1 reshape.272
  11.2 0.6 dynamic_slice.10
  11.8 0.6 compare_convert_fusion.1
  12.5 0.1 slice_reduce_fusion.4
  12.6 0.2 fusion.24
  12.8 0.2 fusion.26
  13.0 12.8 %all_gather.9 = bf16[256,1536]{1,0:T(8,128)(2,1)S(1)} all-gather(bf16[128,1536]{1,0:T(8,128)(2,1)S(1)} %fusion.26), channel_id=1, replica_groups=mesh['req'=16,'mdl'=2] {'mdl'}, dimensions={0}, use_global_device_ids=true | all-gather | bytes 1179648 | tf_op jit(solution)/shard_map/all_gather | solution.py:47
  25.8 0.1 compare_and_fusion
  25.8 0.1 iota_compare_fusion.2
  25.9 76.5 %all-gather.3.cloned.1.call-done = bf16[1536,3352]{1,0:T(8,128)(2,1)} async-done(((bf16[96,3352]{1,0:T(8,128)(2,1)}), bf16[1536,3352]{1,0:T(8,128)(2,1)}) %all-gather.3.cloned.1.call-update) | async-done | bytes 10297360 | tf_op jit(solution)/shard_map/all_gather | solution.py:49
  102.4 8.3 %convolution_convert_fusion = bf16[256,3352]{0,1:T(8,128)(2,1)S(1)} fusion(bf16[256,1536]{1,0:T(8,128)(2,1)S(1)} %all_gather.9, bf16[1536,3352]{1,0:T(8,128)(2,1)} %all-gather.3.cloned.1.call-done), kind=kOutput, calls=%fused_computation.1 | convolution fusion | flops 2636978176 | bytes 12800000 | tf_op jit(solution)/shard_map/dot_general | solution.py:50
  110.7 1.2 copy-done.3
  111.9 0.1 slice.82
  111.9 0.8 copy.63
  112.7 0.2 maximum_convert_fusion
  112.9 1.9 copy.57
  114.8 1.2 multiply_convert_fusion
  116.0 0.0 copy-start.10
  116.0 0.0 copy-start
  116.0 0.1 slice.90
  116.1 1.2 copy.54
  117.3 0.8 compare_select_fusion
  118.1 1.0 multiply_reduce_fusion.1
  119.1 0.8 exponential_multiply_fusion
  119.9 0.0 copy-start.15
  119.9 0.2 fusion.34
  120.1 0.8 fusion.30
  121.0 0.1 copy-done.2
  121.1 3.5 %fusion.10 = f32[2,128,24,64]{1,3,2,0:T(8,128)S(1)} fusion(bf16[2,128,24,64]{1,3,2,0:T(8,128)(2,1)S(1)} %bitcast.75, f32[2,128,24,64]{1,3,2,0:T(8,128)S(1)} %fusion.30, f32[2,128,24]{1,2,0:T(8,128)S(1)} %compare_select_fusion, f32[2,128,24]{1,2,0:T(8,128)S(1)} %get-tuple-element.13, f32[2,128,128]{2,1,0:T(8,128)S(1)} %fusion.34, ...), kind=kOutput, calls=%fused_computation.22 | convolution fusion | flops 609091584 | bytes 4153440 | tf_op jit(solution)/shard_map/gtsh,gshp->gthp/dot_general | solution.py:83
  124.6 0.0 copy-start.11
  124.6 1.2 copy.56
  125.8 30.4 %all-gather.5.cloned.1.call-done = bf16[1536,1536]{0,1:T(8,128)(2,1)} async-done(((bf16[1536,96]{0,1:T(8,128)(2,1)}), bf16[1536,1536]{0,1:T(8,128)(2,1)}) %all-gather.5.cloned.1.call-update) | async-done | bytes 4718608 | tf_op jit(solution)/shard_map/all_gather | solution.py:95
  156.2 5.3 %convolution_convert_fusion.1 = bf16[256,1536]{1,0:T(8,128)(2,1)} fusion(bf16[1536,1536]{0,1:T(8,128)(2,1)} %all-gather.5.cloned.1.call-done, f32[1536]{0:T(1024)S(1)} %copy-done.11, f32[192,8,2,128]{3,2,1,0:T(2,128)S(1)} %bitcast.71, bf16[256,3352]{0,1:T(8,128)(2,1)} %copy-done.3), kind=kOutput, calls=%fused_computation.8 | convolution fusion | flops 1211498496 | bytes 7870464 | tf_op jit(solution)/shard_map/dot_general | solution.py:93
  161.5 0.0 reduce-scatter.2.cloned.1.call-update
  161.6 1.4 gather_fusion
  163.0 0.1 broadcast_select_fusion
  163.2 0.1 convert_element_type.121
  163.3 0.7 convert_element_type.123
  164.0 3.3 %all-to-all-start.1 = ((bf16[2,24,192]{2,1,0:T(8,128)(2,1)}), bf16[2,24,192]{2,1,0:T(8,128)(2,1)S(1)}, u32[]{:S(2)}, u32[]{:S(2)}) async-start(bf16[2,24,192]{2,1,0:T(8,128)(2,1)} %convert_element_type.123), calls=%async_computation.2 | async-start | bytes 49152 | tf_op jit(solution)/shard_map/all_to_all | solution.py:129
  167.3 1.7 multiply_reduce_fusion
  168.9 5.0 %psum.7 = f32[256]{0:T(256)S(1)} all-reduce(f32[256]{0:T(256)S(1)} %multiply_reduce_fusion), channel_id=1, replica_groups=mesh['req'=16,'mdl'=2] {'mdl'}, use_global_device_ids=true, to_apply=%region_3.4 | all-reduce | flops 256 | bytes 2048 | tf_op jit(solution)/shard_map/psum | solution.py:91
  173.9 2.1 %add_convert_fusion = bf16[2,24,64,128]{3,2,1,0:T(8,128)(2,1)S(1)} fusion(f32[2,24,64,128]{3,2,1,0:T(8,128)S(1)} %copy-done, bf16[2,128,24,64]{1,3,2,0:T(8,128)(2,1)} %bitcast.74, f32[2,128,24]{1,2,0:T(8,128)S(1)} %get-tuple-element.8, f32[2,24]{1,0:T(2,128)S(1)} %exp.41, bf16[2,128,1792]{2,1,0:T(8,128)(2,1)} %copy-done.1), kind=kOutput, calls=%fused_computation.29 | convolution fusion | flops 605945856 | bytes 3236032 | tf_op jit(solution)/shard_map/gsh,gshp,gsn->ghpn/dot_general | solution.py:111
  176.1 1.2 convert_element_type.118
  177.3 0.1 dynamic_slice.9
  177.4 0.0 all-to-all-done.1
  177.4 3.5 %all-to-all-start = ((bf16[2,24,8192]{2,1,0:T(8,128)(2,1)}), bf16[2,24,8192]{2,1,0:T(8,128)(2,1)S(1)}, u32[]{:S(2)}, u32[]{:S(2)}) async-start(bf16[2,24,8192]{2,1,0:T(8,128)(2,1)} %convert_element_type.118), calls=%async_computation.1 | async-start | bytes 1572864 | tf_op jit(solution)/shard_map/all_to_all | solution.py:122
  180.9 0.1 convert_element_type.124
  181.0 0.1 concatenate.34
  181.1 0.6 pad_maximum_fusion.1
  181.8 9.9 %all-to-all-done = bf16[2,24,8192]{2,1,0:T(8,128)(2,1)S(1)} async-done(((bf16[2,24,8192]{2,1,0:T(8,128)(2,1)}), bf16[2,24,8192]{2,1,0:T(8,128)(2,1)S(1)}, u32[]{:S(2)}, u32[]{:S(2)}) %all-to-all-start) | async-done | bytes 786464 | tf_op jit(solution)/shard_map/all_to_all | solution.py:122
  191.7 1.3 copy.66
  193.0 2.0 multiply_convert_fusion.3
  (40 shorter events, 0.2 us)
Async XLA Ops:
  7.2 3.8 %copy-start.6 = (bf16[2,3,1536]{2,0,1:T(2,128)(2,1)S(1)}, bf16[2,3,1536]{2,0,1:T(2,128)(2,1)}, u32[]{:S(2)}) copy-start(bf16[2,3,1536]{2,0,1:T(2,128)(2,1)} %param.32) | copy-start | bytes 55300
  7.2 3.8 %copy-start.9 = (bf16[2,3,256]{2,0,1:T(2,128)(2,1)S(1)}, bf16[2,3,256]{2,0,1:T(2,128)(2,1)}, u32[]{:S(2)}) copy-start(bf16[2,3,256]{2,0,1:T(2,128)(2,1)} %param.33) | copy-start | bytes 9220
  7.2 3.8 %copy-start.12 = (f32[24]{0:T(128)S(1)}, f32[24]{0:T(128)}, u32[]{:S(2)}) copy-start(f32[24]{0:T(128)} %param.27) | copy-start | bytes 292
  7.2 3.9 %copy-start.14 = (s32[2]{0:T(128)S(1)}, s32[2]{0:T(128)}, u32[]{:S(2)}) copy-start(s32[2]{0:T(128)} %param.35) | copy-start | bytes 28
  7.2 4.0 %copy-start.13 = (s32[2]{0:T(128)S(1)}, s32[2]{0:T(128)}, u32[]{:S(2)}) copy-start(s32[2]{0:T(128)} %param.34) | copy-start | bytes 28
  7.2 5.3 %copy-start.5 = (f32[5,1536]{1,0:T(8,128)S(1)}, f32[5,1536]{1,0:T(8,128)}, u32[]{:S(2)}) copy-start(f32[5,1536]{1,0:T(8,128)} %param.24) | copy-start | bytes 92164
  7.2 5.3 %copy-start.8 = (f32[5,256]{1,0:T(8,128)S(1)}, f32[5,256]{1,0:T(8,128)}, u32[]{:S(2)}) copy-start(f32[5,256]{1,0:T(8,128)} %param.25) | copy-start | bytes 15364
  7.2 5.4 %copy-start.4 = (bf16[128,1536]{1,0:T(8,128)(2,1)S(1)}, bf16[128,1536]{1,0:T(8,128)(2,1)}, u32[]{:S(2)}) copy-start(bf16[128,1536]{1,0:T(8,128)(2,1)} %param.18) | copy-start | bytes 1179652
  7.2 5.6 %copy-start.7 = (f32[1536]{0:T(1024)S(1)}, f32[1536]{0:T(1024)}, u32[]{:S(2)}) copy-start(f32[1536]{0:T(1024)} %param.19) | copy-start | bytes 18436
  7.3 95.1 %all-gather.3.cloned.1.call-start = ((), (), s32[]{:S(2)}) async-start(), calls=%async_computation.3 | async-start | bytes 11280384 | tf_op jit(solution)/shard_map/all_gather | solution.py:49
  10.2 146.1 %all-gather.5.cloned.1.call-start = ((), (), s32[]{:S(2)}) async-start(), calls=%async_computation.4 | async-start | bytes 5013504 | tf_op jit(solution)/shard_map/all_gather | solution.py:95
  10.9 182.1 %reduce-scatter.2.cloned.1.call-start = ((), (), s32[]{:S(2)}) async-start(), calls=%async_computation.5 | async-start | bytes 1179648 | tf_op jit(solution)/shard_map/reduce_scatter | solution.py:98
  110.6 1.2 copy-start.3
  116.0 4.1 %copy-start.1 = (bf16[2,128,1792]{2,1,0:T(8,128)(2,1)}, bf16[2,128,1792]{2,1,0:T(8,128)(2,1)S(1)}, u32[]{:S(2)}) copy-start(bf16[2,128,1792]{2,1,0:T(8,128)(2,1)S(1)} %multiply_convert_fusion) | copy-start | bytes 2752516
  116.0 1.3 copy-start.10
  116.0 4.1 %copy-start = (f32[2,24,64,128]{3,2,1,0:T(8,128)S(1)}, f32[2,24,64,128]{3,2,1,0:T(8,128)}, u32[]{:S(2)}) copy-start(f32[2,24,64,128]{3,2,1,0:T(8,128)} %param.31) | copy-start | bytes 4718596
  119.9 1.1 copy-start.2
  119.9 1.1 copy-start.15
  124.6 31.7 %copy-start.11 = (f32[1536]{0:T(1024)S(1)}, f32[1536]{0:T(1024)}, u32[]{:S(2)}) copy-start(f32[1536]{0:T(1024)} %param.29) | copy-start | bytes 18436
  164.0 13.4 %all-to-all-start.1 = ((bf16[2,24,192]{2,1,0:T(8,128)(2,1)}), bf16[2,24,192]{2,1,0:T(8,128)(2,1)S(1)}, u32[]{:S(2)}, u32[]{:S(2)}) async-start(bf16[2,24,192]{2,1,0:T(8,128)(2,1)} %convert_element_type.123), calls=%async_computation.2 | async-start | bytes 49152 | tf_op jit(solution)/shard_map/all_to_all | solution.py:129
  177.4 14.3 %all-to-all-start = ((bf16[2,24,8192]{2,1,0:T(8,128)(2,1)}), bf16[2,24,8192]{2,1,0:T(8,128)(2,1)S(1)}, u32[]{:S(2)}, u32[]{:S(2)}) async-start(bf16[2,24,8192]{2,1,0:T(8,128)(2,1)} %convert_element_type.118), calls=%async_computation.1 | async-start | bytes 1572864 | tf_op jit(solution)/shard_map/all_to_all | solution.py:122
Sparse Core Ops, SparseCore 0:
  10.9 91.3 all-gather.2
  104.6 51.5 all-gather.4
  161.7 16.3 reduce-scatter.1

commit v2 on v1

--- a/solution.py
+++ b/solution.py
@@ -1,10 +1,188 @@
 import jax
 import jax.numpy as jnp
 from jax import lax
+from jax.experimental import pallas as pl
+from jax.experimental.pallas import tpu as pltpu
 from jax.sharding import PartitionSpec as P
 
 EPSILON = 1e-05
 HIGHEST = lax.Precision.HIGHEST
+MESH = pl.DeviceIdType.MESH
+CHUNK = 16
+
+
+def ring_fits(rows):
+    return (
+        lax.axis_size("mdl") == 2
+        and lax.axis_size("req") % 4 == 0
+        and lax.axis_size("req") >= 8
+        and rows % (2 * CHUNK) == 0
+    )
+
+
+def ring_kernel(
+    count,
+    own_ref,
+    turned_ref,
+    normed_ref,
+    packed_ref,
+    out_ref,
+    whole_ref,
+    send_sem,
+    recv_sem,
+    twin_send,
+    twin_recv,
+    pair_sem,
+    local_sem,
+):
+    chips = count // 2
+    depth = chips // 2
+    me = lax.axis_index("req")
+    side = lax.axis_index("mdl")
+    core = me % 2
+    chip = me // 2
+    x = chip % 2
+    z = chip // 2
+    place = z + x * (chips - 1 - 2 * z)
+
+    def at(spot, which):
+        spot = (spot + 2 * chips) % chips
+        far = spot // depth
+        level = spot + far * (chips - 1 - 2 * spot)
+        return (level * 2 + far) * 2 + which
+
+    right, left, twin = at(place + 1, core), at(place - 1, core), at(place, 1 - core)
+    partner = 1 - side
+    barrier = pltpu.get_barrier_semaphore()
+    for other in (right, left, twin):
+        pl.semaphore_signal(barrier, inc=1, device_id=(other, side), device_id_type=MESH)
+    pl.semaphore_signal(barrier, inc=1, device_id=(me, partner), device_id_type=MESH)
+    pl.semaphore_wait(barrier, 4)
+
+    half = own_ref.shape[0] // 2
+    pieces = [("p", k * CHUNK, CHUNK) for k in range(half // CHUNK)] + [("o", 0, half)]
+
+    def views(owner, way, piece, first):
+        kind, start, size = piece
+        rows = pl.ds(way * half + start, size)
+        target = (packed_ref if kind == "p" else out_ref).at[owner, rows]
+        if first:
+            return (own_ref if kind == "p" else turned_ref).at[rows], target
+        return target, target
+
+    def hop(way, step, k):
+        owner = at(place - step if way == 0 else place + step, core)
+        source, target = views(owner, way, pieces[k], step == 0)
+        return pltpu.make_async_remote_copy(
+            src_ref=source,
+            dst_ref=target,
+            send_sem=send_sem.at[way, step, k],
+            recv_sem=recv_sem.at[way, step, k],
+            device_id=(right if way == 0 else left, side),
+            device_id_type=MESH,
+        )
+
+    def across(way, step, k):
+        owner = at(place - step if way == 0 else place + step, core)
+        source, target = views(owner, way, pieces[k], step == 0)
+        return pltpu.make_async_remote_copy(
+            src_ref=source,
+            dst_ref=target,
+            send_sem=twin_send.at[way, step, k],
+            recv_sem=twin_recv.at[way, step, k],
+            device_id=(twin, side),
+            device_id_type=MESH,
+        )
+
+    started = []
+    for k in range(len(pieces)):
+        for way in range(2):
+            copy = hop(way, 0, k)
+            copy.start()
+            started.append(copy)
+    rows_copy = pltpu.make_async_remote_copy(
+        src_ref=normed_ref,
+        dst_ref=whole_ref.at[side],
+        send_sem=pair_sem.at[0],
+        recv_sem=pair_sem.at[1],
+        device_id=(me, partner),
+        device_id_type=MESH,
+    )
+    rows_copy.start()
+    locals_ = [
+        pltpu.make_async_copy(own_ref, packed_ref.at[me], local_sem.at[0]),
+        pltpu.make_async_copy(turned_ref, out_ref.at[me], local_sem.at[1]),
+        pltpu.make_async_copy(normed_ref, whole_ref.at[side], local_sem.at[2]),
+    ]
+    for copy in locals_:
+        copy.start()
+    crossed = []
+    for step in range(chips):
+        for k in range(len(pieces)):
+            for way in range(2):
+                if step > 0:
+                    hop(way, step - 1, k).wait_recv()
+                    if step < chips - 1:
+                        copy = hop(way, step, k)
+                        copy.start()
+                        started.append(copy)
+                copy = across(way, step, k)
+                copy.start()
+                crossed.append(copy)
+    for copy in locals_:
+        copy.wait()
+    for copy in started:
+        copy.wait_send()
+    for copy in crossed:
+        copy.wait()
+    rows_copy.wait()
+
+
+def ring_gather(packed, turned, normed):
+    count = lax.axis_size("req")
+    chips = count // 2
+    parts = packed.shape[0] // (2 * CHUNK) + 1
+    anywhere = pl.BlockSpec(memory_space=pl.ANY)
+    gathered, columns, whole = pl.pallas_call(
+        lambda *refs: ring_kernel(count, *refs),
+        out_shape=(
+            jax.ShapeDtypeStruct((count,) + packed.shape, packed.dtype),
+            jax.ShapeDtypeStruct((count,) + turned.shape, turned.dtype),
+            jax.ShapeDtypeStruct((2,) + normed.shape, normed.dtype),
+        ),
+        in_specs=[anywhere] * 3,
+        out_specs=(anywhere,) * 3,
+        scratch_shapes=[
+            pltpu.SemaphoreType.DMA((2, chips - 1, parts)),
+            pltpu.SemaphoreType.DMA((2, chips - 1, parts)),
+            pltpu.SemaphoreType.DMA((2, chips, parts)),
+            pltpu.SemaphoreType.DMA((2, chips, parts)),
+            pltpu.SemaphoreType.DMA((2,)),
+            pltpu.SemaphoreType.DMA((3,)),
+        ],
+        compiler_params=pltpu.CompilerParams(collective_id=0, has_side_effects=True),
+    )(packed, turned, normed)
+    return (
+        gathered.reshape(-1, packed.shape[1]),
+        columns.reshape(-1, turned.shape[1]),
+        whole.reshape(-1, normed.shape[1]),
+    )
+
+
+def gather_all(packed, out_proj, normed):
+    if ring_fits(packed.shape[0]):
+        spare = -packed.shape[1] % 128
+        packed = jnp.pad(packed, ((0, 0), (0, spare)))
+        return ring_gather(packed, out_proj.T, normed)
+    return (
+        lax.all_gather(packed, "req", axis=0, tiled=True),
+        lax.all_gather(out_proj.T, "req", axis=0, tiled=True),
+        lax.all_gather(normed, "mdl", axis=0, tiled=True),
+    )
+
+
+def swap(array):
+    return lax.ppermute(array, "mdl", [(0, 1), (1, 0)])
 
 
 def local(
@@ -44,14 +222,14 @@
     first_end = widths[0]
     second_end = first_end + widths[1]
     third_end = second_end + widths[2]
-    whole = lax.all_gather(normed, "mdl", axis=0, tiled=True)
+    fourth_end = third_end + widths[3]
     packed = jnp.concatenate((gate_proj, value_proj, state_proj, step_proj), 1)
-    joined_piece = lax.all_gather(packed, "req", axis=0, tiled=True)
+    joined_piece, out_turned, whole = gather_all(packed, out_proj, normed)
     joined = jnp.dot(whole, joined_piece, preferred_element_type=jnp.float32)
     gates = joined[:, :first_end].astype(jnp.bfloat16)
     values = joined[:, first_end:second_end].astype(jnp.bfloat16)
     readers = joined[:, second_end:third_end].astype(jnp.bfloat16)
-    step_raw = joined[:, third_end:].astype(jnp.bfloat16)
+    step_raw = joined[:, third_end:fourth_end].astype(jnp.bfloat16)
     current = jnp.concatenate([values, readers], 1).reshape(requests, span, -1)
     edges = jnp.concatenate([edge_value, edge_state], 2)
     extended = jnp.concatenate([edges, current], 1).astype(jnp.float32)
@@ -88,16 +266,22 @@
     product = outputs.reshape(group_rows, inner_here) * jax.nn.silu(gates.astype(jnp.float32))
     squares = jnp.sum(product * product, -1)
     gated = (product * output_gain).astype(jnp.bfloat16)
-    total_squares = lax.psum(squares, "mdl")
+    paired = lax.axis_size("mdl") == 2
+    total_squares = squares + swap(squares) if paired else lax.psum(squares, "mdl")
     scale = lax.rsqrt(total_squares / (inner_here * lax.axis_size("mdl")) + EPSILON)
-    partial_terms = jnp.dot(
-        gated,
-        lax.all_gather(out_proj, "req", axis=1, tiled=True),
-        preferred_element_type=jnp.float32,
-    )
-    mine = lax.psum_scatter(
-        partial_terms.astype(jnp.bfloat16), "mdl", scatter_dimension=0, tiled=True
-    ).astype(jnp.float32)
+    partial_terms = lax.dot_general(
+        gated, out_turned, (((1,), (1,)), ((), ())), preferred_element_type=jnp.float32
+    ).astype(jnp.bfloat16)
+    if paired:
+        theirs = lax.dynamic_slice_in_dim(
+            partial_terms, (1 - my_index) * rows_dev, rows_dev, 0
+        )
+        mine = lax.dynamic_slice_in_dim(partial_terms, my_index * rows_dev, rows_dev, 0)
+        mine = mine.astype(jnp.float32) + swap(theirs).astype(jnp.float32)
+    else:
+        mine = lax.psum_scatter(
+            partial_terms, "mdl", scatter_dimension=0, tiled=True
+        ).astype(jnp.float32)
     my_scale = lax.dynamic_slice_in_dim(scale, my_index * rows_dev, rows_dev, 0)
     my_lengths = lax.dynamic_slice_in_dim(lengths, my_index * here_count, here_count, 0)
     live = (positions[None, :] < my_lengths[:, None]).reshape(rows_dev).astype(jnp.float32)
@@ -114,28 +298,40 @@
     state_here = jnp.exp(running_last)[:, :, None, None] * state_start + gathered_state
     picks = accepted[:, None] + jnp.arange(edge_count, dtype=jnp.int32)[None, :]
     selected = jnp.take_along_axis(extended, picks[:, :, None], axis=1)
-    value_edges = selected[..., :inner_here].reshape(requests, edge_count, heads_here, head_dim)
-    value_edges = value_edges.transpose(0, 2, 1, 3).reshape(
-        requests, heads_here, edge_count * head_dim
-    )
-    states_home, edges_home = (
-        lax.all_to_all(
-            state_here.reshape(requests, heads_here, head_dim * nstate).astype(jnp.bfloat16),
-            "mdl",
-            split_axis=0,
-            concat_axis=1,
-            tiled=True,
-        ).astype(jnp.float32),
-        lax.all_to_all(
-            value_edges.astype(jnp.bfloat16), "mdl", split_axis=0, concat_axis=1, tiled=True
-        ).astype(value_edges.dtype),
-    )
-    heads_all = states_home.shape[1]
-    state_final = states_home.reshape(here_count, heads_all, head_dim, nstate)
-    edges_home = edges_home.reshape(here_count, heads_all, edge_count, head_dim).transpose(
-        0, 2, 1, 3
-    )
-    edges_home = edges_home.reshape(here_count, edge_count, heads_all * head_dim)
+    if paired:
+        def to_owner(array, kind):
+            sent = lax.dynamic_slice_in_dim(array, (1 - my_index) * here_count, here_count, 0)
+            kept = lax.dynamic_slice_in_dim(array, my_index * here_count, here_count, 0)
+            come = swap(sent.astype(jnp.bfloat16)).astype(kind)
+            kept = kept.astype(kind)
+            first = my_index == 0
+            return jnp.where(first, kept, come), jnp.where(first, come, kept)
+
+        state_final = jnp.concatenate(to_owner(state_here, jnp.float32), 1)
+        edges_home = jnp.concatenate(to_owner(selected[..., :inner_here], selected.dtype), 2)
+    else:
+        value_edges = selected[..., :inner_here].reshape(requests, edge_count, heads_here, head_dim)
+        value_edges = value_edges.transpose(0, 2, 1, 3).reshape(
+            requests, heads_here, edge_count * head_dim
+        )
+        states_home, edges_home = (
+            lax.all_to_all(
+                state_here.reshape(requests, heads_here, head_dim * nstate).astype(jnp.bfloat16),
+                "mdl",
+                split_axis=0,
+                concat_axis=1,
+                tiled=True,
+            ).astype(jnp.float32),
+            lax.all_to_all(
+                value_edges.astype(jnp.bfloat16), "mdl", split_axis=0, concat_axis=1, tiled=True
+            ).astype(value_edges.dtype),
+        )
+        heads_all = states_home.shape[1]
+        state_final = states_home.reshape(here_count, heads_all, head_dim, nstate)
+        edges_home = edges_home.reshape(here_count, heads_all, edge_count, head_dim).transpose(
+            0, 2, 1, 3
+        )
+        edges_home = edges_home.reshape(here_count, edge_count, heads_all * head_dim)
     state_edges = lax.dynamic_slice_in_dim(
         selected[..., inner_here:], my_index * here_count, here_count, 0
     )

time: 202 us -> 154 us (0.76)
  waiting for transfers between devices: 118 us -> 3.53 us
  Pallas kernels: 0 us -> 80.9 us
  blocking collectives: 17.7 us -> 0 us
  between operations: 14.2 us -> 0.86 us
  local copies, waits for them, and re-layouts: 13.4 us -> 20.9 us
  other arithmetic: 10.6 us -> 16.8 us
  matrix products: 21.2 us -> 25.7 us
  starting transfers between devices: 6.91 us -> 4.2 us
    all_gather x2 -> x0, waiting for transfers between devices: 107 us -> none  [the longest x1 76.5 us: local(): joined_piece = lax.all_gather(packed, 'req', axis=0, tiled=True)]
    pallas_call x0 -> x1, Pallas kernels: none -> 80.9 us  [ring_gather(): pl.pallas_call(lambda *refs: ring_kernel(count, *refs), out_shape=(jax.Sh...]
    all_gather x1 -> x0, blocking collectives: 12.8 us -> none  [local(): whole = lax.all_gather(normed, 'mdl', axis=0, tiled=True)]
    all_to_all x2 -> x0, waiting for transfers between devices: 9.9 us -> none  [the longest x1 9.9 us: local(): lax.all_to_all(state_here.reshape(requests, heads_here, head_dim * nstate...]
    reshape x1 -> x3, local copies, waits for them, and re-layouts: 0.8 us -> 7.74 us  [the longest x2 6.85 us: local(): outputs.reshape(group_rows, inner_here)]
    all_to_all x2 -> x0, starting transfers between devices: 6.79 us -> none  [the longest x1 3.54 us: local(): lax.all_to_all(state_here.reshape(requests, heads_here, head_dim * nstate...]
    psum x1 -> x0, blocking collectives: 4.99 us -> none  [local(): total_squares = lax.psum(squares, 'mdl')]
    ppermute x0 -> x4, starting transfers between devices: none -> 4.2 us  [swap(): return lax.ppermute(array, 'mdl', [(0, 1), (1, 0)])]
  transfers between devices with their start and end apart: 5 -> 4, of which waited for: 3 -> 1; matrix products, arithmetic and copies ran while one was open for 17% -> 11% of each run, Pallas kernels for 0% -> 0%
where the time goes in v2:
time: 154 us; the launch traced here: 153 us
  Pallas kernels  80.9 us (53%)
  matrix products  25.7 us (17%)
  local copies, waits for them, and re-layouts  20.9 us (14%)
  other arithmetic  16.8 us (11%)
  starting transfers between devices  4.2 us (3%)
  waiting for transfers between devices  3.53 us (2%)
    pallas_call x1, Pallas kernels, ring_gather(): pl.pallas_call(lambda *refs: ring_kernel(count, *refs), out_shape=(jax.Sh...  80.9 us
    dot_general x1, matrix products, local(): joined = jnp.dot(whole, joined_piece, preferred_element_type=jnp.float32)  7.29 us
    reshape x2, local copies, waits for them, and re-layouts, local(): outputs.reshape(group_rows, inner_here)  6.85 us
    dot_general x1, matrix products, local(): outputs = jnp.einsum('gtsh,gshp->gthp', kernel, vals_f, precision=HIGHEST)  6.6 us
    dot_general x1, matrix products, local(): lax.dot_general(gated, out_turned, (((1,), (1,)), ((), ())), preferred_el...  4.64 us
    ppermute x4, starting transfers between devices, swap(): return lax.ppermute(array, 'mdl', [(0, 1), (1, 0)])  4.2 us
    ppermute x4, waiting for transfers between devices, swap(): return lax.ppermute(array, 'mdl', [(0, 1), (1, 0)])  3.53 us
    dot_general x1, matrix products, local(): jnp.einsum('gsh,gshp,gsn->ghpn', weights_s, vals_f, inputs_b.astype(jnp.f...  3.28 us
  transfers between devices with their start and end apart: 4, of which 1 were waited for; matrix products, arithmetic and copies ran while one was open for 11% of the time, Pallas kernels for 0%

profile of v2, /device:TPU:0, one launch (start us, length us, event | category | flops | bytes accessed | tf_op | source)
XLA Modules:
  0.0 153.0 jit_solution(17436273171682456483)
XLA Ops:
  0.6 0.8 copy.30
  1.4 1.2 fusion.28
  2.6 1.9 %fusion.30.refs_2_ = bf16[128,1536]{1,0:T(8,128)(2,1)} fusion(bf16[128,1536]{1,0:T(8,128)(2,1)} %param.18, f32[1536]{0:T(1024)} %param.19, f32[128]{0:T(128)S(1)} %add_rsqrt_fusion.1), kind=kLoop, calls=%fused_computation.52 | loop fusion | flops 786432 | bytes 793088 | tf_op jit(solution)/shard_map/convert_element_type | solution.py:220
  4.5 2.0 %fusion.35.refs_0_ = bf16[96,3456]{1,0:T(8,128)(2,1)} fusion(bf16[96,24]{1,0:T(8,128)(2,1)S(1)} %copy.30, bf16[96,256]{1,0:T(8,128)(2,1)} %param.22, bf16[96,1536]{1,0:T(8,128)(2,1)} %param.21, bf16[96,1536]{1,0:T(8,128)(2,1)} %param.20), kind=kLoop, calls=%fused_computation.59 | loop fusion | flops 4313088 | bytes 1307136 | tf_op jit(solution)/shard_map/concatenate | solution.py:226
  6.5 80.9 %shard_map.193 = (bf16[16,96,3456]{2,1,0:T(8,128)(2,1)}, bf16[16,96,1536]{2,1,0:T(8,128)(2,1)}, bf16[2,128,1536]{2,1,0:T(8,128)(2,1)}) custom-call(bf16[96,3456]{1,0:T(8,128)(2,1)} %fusion.35.refs_0_, bf16[96,1536]{1,0:T(8,128)(2,1)} %bitcast.42, bf16[128,1536]{1,0:T(8,128)(2,1)} %fusion.30.refs_2_), custom_call_target="tpu_custom_call" | custom-call | tf_op jit(solution)/shard_map/pallas_call | solution.py:146
  87.3 7.3 %convolution_convert_fusion = bf16[256,3456]{1,0:T(8,128)(2,1)S(1)} fusion(bf16[256,1536]{1,0:T(8,128)(2,1)} %bitcast.46, bf16[1536,3456]{1,0:T(8,128)(2,1)} %bitcast.44), kind=kOutput, calls=%fused_computation.1 | convolution fusion | flops 2718793728 | bytes 13172736 | tf_op jit(solution)/shard_map/dot_general | solution.py:228
  94.6 0.0 copy-start.11
  94.7 0.0 copy-start.9
  94.7 0.0 copy-start.8
  94.7 0.0 copy-start.10
  94.7 0.1 slice.81
  94.8 0.6 slice.92
  95.4 0.1 copy-done.9
  95.5 0.1 copy-done.8
  95.6 0.1 slice_reduce_fusion.4
  95.7 0.2 copy-done.4
  95.9 0.2 maximum_convert_fusion
  96.1 1.2 multiply_convert_fusion
  97.3 0.0 copy-start
  97.3 0.9 slice.89
  98.2 0.2 copy-done.3
  98.5 0.8 fusion.41
  99.3 0.6 iota_compare_fusion.1
  99.9 2.3 %copy.31 = bf16[2,128,1536]{1,2,0:T(8,128)(2,1)} copy(bf16[2,128,1536]{2,1,0:T(8,128)(2,1)} %slice.89) | data formatting | bytes 1572864 | tf_op jit(solution)/shard_map/slice | solution.py:243
  102.2 2.8 %fusion.37 = f32[2,128,24,64]{1,3,2,0:T(8,128)} fusion(f32[2,24,64,128]{3,2,1,0:T(8,128)S(1)} %copy-done, bf16[2,128,1792]{2,1,0:T(8,128)(2,1)} %copy-done.3), kind=kOutput, calls=%fused_computation.62 | convolution fusion | flops 603979776 | bytes 3211264 | tf_op jit(solution)/shard_map/gtn,ghpn->gthp/dot_general | solution.py:262
  105.0 0.9 copy.32
  105.9 0.7 broadcast_add_fusion
  106.6 0.1 iota_compare_fusion.3
  106.7 0.1 compare_select_fusion
  106.8 0.3 multiply_reduce_fusion.1
  107.1 0.7 exponential_multiply_fusion
  107.8 6.6 %fusion.10 = f32[2,128,24,64]{1,3,2,0:T(8,128)} fusion(bf16[2,128,24,64]{1,3,2,0:T(8,128)(2,1)} %bitcast.40, f32[2,128,24,64]{1,3,2,0:T(8,128)} %fusion.37, f32[2,128,24]{1,2,0:T(8,128)S(1)} %compare_select_fusion, f32[2,128,24]{1,2,0:T(8,128)S(1)} %get-tuple-element.23, f32[2,128,128]{2,1,0:T(8,128)} %fusion.41, pred[128,128]{1,0:T(8,128)(4,1)} %iota_compare_fusion.1, ...), kind=kOutput, calls=%fused_computation.22 | convolution fusion | flops 609091584 | bytes 4153440 | tf_op jit(solution)/shard_map/gtsh,gshp->gthp/dot_general | solution.py:261
  114.4 3.3 %copy.38 = f32[2,128,24,64]{3,2,1,0:T(8,128)} copy(f32[2,128,24,64]{1,3,2,0:T(8,128)} %fusion.10) | data formatting | bytes 3145728 | tf_op jit(solution)/shard_map/reshape | solution.py:266
  117.7 3.6 %reshape.254 = f32[256,1536]{1,0:T(8,128)} reshape(f32[2,128,24,64]{3,2,1,0:T(8,128)} %copy.38) | data formatting | bytes 3145728 | tf_op jit(solution)/shard_map/reshape | solution.py:266
  121.3 4.6 %convolution_convert_fusion.1 = bf16[256,1536]{1,0:T(8,128)(2,1)S(1)} fusion(bf16[1536,1536]{1,0:T(8,128)(2,1)} %bitcast.45, f32[1536]{0:T(1024)S(1)} %copy-done.13, f32[256,1536]{1,0:T(8,128)} %reshape.254, bf16[256,3456]{1,0:T(8,128)(2,1)} %copy-done.4), kind=kOutput, calls=%fused_computation.8 | convolution fusion | flops 1211498496 | bytes 7870464 | tf_op jit(solution)/shard_map/dot_general | solution.py:272
  125.9 0.0 copy-start.7
  125.9 0.8 constant_dynamic-slice_fusion
  126.8 1.5 %collective-permute-start = (bf16[128,1536]{1,0:T(8,128)(2,1)}, bf16[128,1536]{1,0:T(8,128)(2,1)}, u32[]{:S(2)}, u32[]{:S(2)}) collective-permute-start(bf16[128,1536]{1,0:T(8,128)(2,1)} %constant_dynamic-slice_fusion), channel_id=1, source_target_pairs={{0,1},{1,0},{2,3},{3,2},{4,5},{5,4},{6,7},{7,6},{8,9},{9,8},{10,11... | collective-permute-start | bytes 1179656 | tf_op jit(solution)/shard_map/ppermute | solution.py:185
  128.3 1.7 %multiply_reduce_fusion = f32[256]{0:T(256)S(1)} fusion(f32[256,1536]{1,0:T(8,128)S(1)} %copy-done.1, bf16[256,3456]{1,0:T(8,128)(2,1)} %copy-done.4), kind=kLoop, calls=%fused_computation.31 | loop fusion | flops 3145472 | bytes 2360320 | tf_op jit(solution)/shard_map/reduce_sum | solution.py:267
  130.0 0.6 collective-permute-start.1
  130.6 0.6 exp.41
  131.2 3.3 %multiply_add_fusion = f32[2,24,64,128]{3,2,1,0:T(8,128)} fusion(f32[2,24,64,128]{3,2,1,0:T(8,128)S(1)} %copy-done, bf16[2,128,24,64]{1,3,2,0:T(8,128)(2,1)} %bitcast.41, f32[2,128,24]{1,2,0:T(8,128)S(1)} %copy-done.7, f32[2,24]{1,0:T(2,128)} %exp.41, bf16[2,128,1792]{2,1,0:T(8,128)(2,1)} %copy-done.3), kind=kOutput, calls=%fused_computation.30 | convolution fusion | flops 605552640 | bytes 4023296 | tf_op jit(solution)/shard_map/gsh,gshp,gsn->ghpn/dot_general | solution.py:295
  134.5 2.0 %dynamic-slice_convert_fusion = bf16[1,24,64,128]{3,2,1,0:T(8,128)(2,1)} fusion(f32[2,24,64,128]{3,2,1,0:T(8,128)} %multiply_add_fusion, s32[]{:T(128)S(6)} %select_n.84), kind=kLoop, calls=%fused_computation.53 | loop fusion | bytes 786436 | tf_op jit(solution)/shard_map/convert_element_type | solution.py:305
  136.4 1.5 collective-permute-start.2
  138.0 1.9 %copy.35 = bf16[2,131,1792]{2,0,1:T(2,128)(2,1)} copy(f32[2,131,1792]{2,1,0:T(8,128)S(1)} %maximum_convert_fusion) | data formatting | bytes 2817024 | tf_op jit(solution)/shard_map/convert_element_type | solution.py:235
  139.9 0.1 fusion.52
  139.9 0.1 compare_and_fusion
  140.0 0.1 reshape.245
  140.1 1.4 gather_fusion
  141.5 0.1 broadcast_select_fusion
  141.7 0.6 collective-permute-start.3
  142.3 0.6 dynamic_slice.30
  142.8 0.6 compare_convert_fusion.1
  143.5 0.0 collective-permute-done.1
  143.5 0.6 add_rsqrt_fusion
  144.1 0.1 dynamic_slice.29
  144.2 3.5 %collective-permute-done.3 = bf16[1,3,1536]{2,1,0:T(4,128)(2,1)S(1)} collective-permute-done((bf16[1,3,1536]{2,1,0:T(4,128)(2,1)S(1)}, bf16[1,3,1536]{2,1,0:T(4,128)(2,1)S(1)}, u32[]{:S(2)}, u32[]{:S(2)}) %collective-permute-start.3) | collective-permute-done | bytes 9248 | tf_op jit(solution)/shard_map/ppermute | solution.py:185
  147.7 0.6 pad_maximum_fusion.1
  148.4 0.0 collective-permute-done.2
  148.4 1.2 convert_select_fusion.1
  149.6 1.2 pad_maximum_fusion
  150.8 0.0 collective-permute-done
  150.8 0.2 copy-done.6
  151.0 2.0 %multiply_convert_fusion.3 = bf16[128,1536]{1,0:T(8,128)(2,1)} fusion(bf16[128,1536]{1,0:T(8,128)(2,1)} %collective-permute-done, f32[128]{0:T(128)S(1)} %compare_convert_fusion.1, f32[128]{0:T(128)S(1)} %dynamic_slice.29, bf16[256,1536]{1,0:T(8,128)(2,1)S(1)} %copy-done.6, s32[]{:T(128)S(6)} %select_n.79), kind=kLoop, calls=%fused_computation.55 | loop fusion | flops 1179648 | bytes 1180676 | tf_op jit(solution)/shard_map/convert_element_type | solution.py:288
  (35 shorter events, 0.2 us)
Async XLA Ops:
  94.6 1.2 copy-start.4
  94.6 0.7 copy-start.11
  94.7 0.8 copy-start.9
  94.7 0.9 copy-start.8
  94.7 0.9 copy-start.10
  97.3 1.2 copy-start.3
  97.3 4.9 %copy-start = (f32[2,24,64,128]{3,2,1,0:T(8,128)S(1)}, f32[2,24,64,128]{3,2,1,0:T(8,128)}, u32[]{:S(2)}) copy-start(f32[2,24,64,128]{3,2,1,0:T(8,128)} %param.31) | copy-start | bytes 4718596
  102.2 4.5 %copy-start.14 = (f32[24]{0:T(128)S(1)}, f32[24]{0:T(128)}, u32[]{:S(2)}) copy-start(f32[24]{0:T(128)} %param.27) | copy-start | bytes 292
  102.2 4.5 %copy-start.12 = (f32[24]{0:T(128)S(1)}, f32[24]{0:T(128)}, u32[]{:S(2)}) copy-start(f32[24]{0:T(128)} %param.26) | copy-start | bytes 292
  117.7 3.6 %copy-start.13 = (f32[1536]{0:T(1024)S(1)}, f32[1536]{0:T(1024)}, u32[]{:S(2)}) copy-start(f32[1536]{0:T(1024)} %param.29) | copy-start | bytes 18436
  121.3 7.1 %copy-start.1 = (f32[256,1536]{1,0:T(8,128)S(1)}, f32[256,1536]{1,0:T(8,128)}, u32[]{:S(2)}) copy-start(f32[256,1536]{1,0:T(8,128)} %reshape.254) | copy-start | bytes 4718596
  125.9 4.1 %copy-start.5 = (bf16[256,1536]{1,0:T(8,128)(2,1)}, bf16[256,1536]{1,0:T(8,128)(2,1)S(1)}, u32[]{:S(2)}) copy-start(bf16[256,1536]{1,0:T(8,128)(2,1)S(1)} %convolution_convert_fusion.1) | copy-start | bytes 2359300
  125.9 5.3 %copy-start.7 = (f32[2,128,24]{1,2,0:T(8,128)S(1)}, f32[2,128,24]{1,2,0:T(8,128)}, u32[]{:S(2)}) copy-start(f32[2,128,24]{1,2,0:T(8,128)} %get-tuple-element.18) | copy-start | bytes 73732
  126.8 24.0 %collective-permute-start = (bf16[128,1536]{1,0:T(8,128)(2,1)}, bf16[128,1536]{1,0:T(8,128)(2,1)}, u32[]{:S(2)}, u32[]{:S(2)}) collective-permute-start(bf16[128,1536]{1,0:T(8,128)(2,1)} %constant_dynamic-slice_fusion), channel_id=1, source_target_pairs={{0,1},{1,0},{2,3},{3,2},{4,5},{5,4},{6,7},{7,6},{8,9},{9,8},{10,11... | collective-permute-start | bytes 1179656 | tf_op jit(solution)/shard_map/ppermute | solution.py:185
  130.0 13.5 %collective-permute-start.1 = (f32[256]{0:T(256)S(1)}, f32[256]{0:T(256)}, u32[]{:S(2)}, u32[]{:S(2)}) collective-permute-start(f32[256]{0:T(256)S(1)} %multiply_reduce_fusion), channel_id=1, source_target_pairs={{0,1},{1,0},{2,3},{3,2},{4,5},{5,4},{6,7},{7,6},{8,9},{9,8},{10,11... | collective-permute-start | bytes 3080 | tf_op jit(solution)/shard_map/ppermute | solution.py:185
  136.4 3.4 %copy-start.15 = (s32[2]{0:T(128)S(1)}, s32[2]{0:T(128)}, u32[]{:S(2)}) copy-start(s32[2]{0:T(128)} %param.35) | copy-start | bytes 28
  136.4 5.8 %copy-start.16 = (s32[2]{0:T(128)S(1)}, s32[2]{0:T(128)}, u32[]{:S(2)}) copy-start(s32[2]{0:T(128)} %param.34) | copy-start | bytes 28
  136.4 11.9 %copy-start.2 = (f32[2,24,64,128]{3,2,1,0:T(8,128)S(1)}, f32[2,24,64,128]{3,2,1,0:T(8,128)}, u32[]{:S(2)}) copy-start(f32[2,24,64,128]{3,2,1,0:T(8,128)} %multiply_add_fusion) | copy-start | bytes 4718596
  136.4 11.9 %collective-permute-start.2 = (bf16[1,24,64,128]{3,2,1,0:T(8,128)(2,1)}, bf16[1,24,64,128]{3,2,1,0:T(8,128)(2,1)}, u32[]{:S(2)}, u32[]{:S(2)}) collective-permute-start(bf16[1,24,64,128]{3,2,1,0:T(8,128)(2,1)} %dynamic-slice_convert_fusion), channel_id=1, source_target_pairs={{0,1},{1,0},{2,3},{3,2},{4,5},{5,4},{6,7},{7,6},{8,9},{9,8},{10,11... | collective-permute-start | bytes 1179656 | tf_op jit(solution)/shard_map/ppermute | solution.py:185
  141.7 6.1 %collective-permute-start.3 = (bf16[1,3,1536]{2,1,0:T(4,128)(2,1)S(1)}, bf16[1,3,1536]{2,1,0:T(4,128)(2,1)S(1)}, u32[]{:S(2)}, u32[]{:S(2)}) collective-permute-start(bf16[1,3,1536]{2,1,0:T(4,128)(2,1)S(1)} %dynamic-slice_convert_fusion.1), channel_id=1, source_target_pairs={{0,1},{1,0},{2,3},{3,2},{4,5},{5,4},{6,7},{7,6},{8,9},{9,8},{10,11... | collective-permute-start | bytes 27656 | tf_op jit(solution)/shard_map/ppermute | solution.py:185
  149.6 1.4 copy-start.6

commit v3 on v2

--- a/solution.py
+++ b/solution.py
@@ -23,10 +23,8 @@
 def ring_kernel(
     count,
     own_ref,
-    turned_ref,
     normed_ref,
     packed_ref,
-    out_ref,
     whole_ref,
     send_sem,
     recv_sem,
@@ -60,15 +58,12 @@
     pl.semaphore_wait(barrier, 4)
 
     half = own_ref.shape[0] // 2
-    pieces = [("p", k * CHUNK, CHUNK) for k in range(half // CHUNK)] + [("o", 0, half)]
+    pieces = [k * CHUNK for k in range(half // CHUNK)]
 
     def views(owner, way, piece, first):
-        kind, start, size = piece
-        rows = pl.ds(way * half + start, size)
-        target = (packed_ref if kind == "p" else out_ref).at[owner, rows]
-        if first:
-            return (own_ref if kind == "p" else turned_ref).at[rows], target
-        return target, target
+        rows = pl.ds(way * half + piece, CHUNK)
+        target = packed_ref.at[owner, rows]
+        return (own_ref.at[rows] if first else target), target
 
     def hop(way, step, k):
         owner = at(place - step if way == 0 else place + step, core)
@@ -111,8 +106,7 @@
     rows_copy.start()
     locals_ = [
         pltpu.make_async_copy(own_ref, packed_ref.at[me], local_sem.at[0]),
-        pltpu.make_async_copy(turned_ref, out_ref.at[me], local_sem.at[1]),
-        pltpu.make_async_copy(normed_ref, whole_ref.at[side], local_sem.at[2]),
+        pltpu.make_async_copy(normed_ref, whole_ref.at[side], local_sem.at[1]),
     ]
     for copy in locals_:
         copy.start()
@@ -138,45 +132,42 @@
     rows_copy.wait()
 
 
-def ring_gather(packed, turned, normed):
+def ring_gather(packed, normed):
     count = lax.axis_size("req")
     chips = count // 2
-    parts = packed.shape[0] // (2 * CHUNK) + 1
+    parts = packed.shape[0] // (2 * CHUNK)
     anywhere = pl.BlockSpec(memory_space=pl.ANY)
-    gathered, columns, whole = pl.pallas_call(
+    gathered, whole = pl.pallas_call(
         lambda *refs: ring_kernel(count, *refs),
         out_shape=(
             jax.ShapeDtypeStruct((count,) + packed.shape, packed.dtype),
-            jax.ShapeDtypeStruct((count,) + turned.shape, turned.dtype),
             jax.ShapeDtypeStruct((2,) + normed.shape, normed.dtype),
         ),
-        in_specs=[anywhere] * 3,
-        out_specs=(anywhere,) * 3,
+        in_specs=[anywhere] * 2,
+        out_specs=(anywhere,) * 2,
         scratch_shapes=[
             pltpu.SemaphoreType.DMA((2, chips - 1, parts)),
             pltpu.SemaphoreType.DMA((2, chips - 1, parts)),
             pltpu.SemaphoreType.DMA((2, chips, parts)),
             pltpu.SemaphoreType.DMA((2, chips, parts)),
             pltpu.SemaphoreType.DMA((2,)),
-            pltpu.SemaphoreType.DMA((3,)),
+            pltpu.SemaphoreType.DMA((2,)),
         ],
         compiler_params=pltpu.CompilerParams(collective_id=0, has_side_effects=True),
-    )(packed, turned, normed)
+    )(packed, normed)
     return (
         gathered.reshape(-1, packed.shape[1]),
-        columns.reshape(-1, turned.shape[1]),
         whole.reshape(-1, normed.shape[1]),
     )
 
 
-def gather_all(packed, out_proj, normed):
+def gather_all(packed, normed):
     if ring_fits(packed.shape[0]):
         spare = -packed.shape[1] % 128
         packed = jnp.pad(packed, ((0, 0), (0, spare)))
-        return ring_gather(packed, out_proj.T, normed)
+        return ring_gather(packed, normed)
     return (
         lax.all_gather(packed, "req", axis=0, tiled=True),
-        lax.all_gather(out_proj.T, "req", axis=0, tiled=True),
         lax.all_gather(normed, "mdl", axis=0, tiled=True),
     )
 
@@ -224,7 +215,8 @@
     third_end = second_end + widths[2]
     fourth_end = third_end + widths[3]
     packed = jnp.concatenate((gate_proj, value_proj, state_proj, step_proj), 1)
-    joined_piece, out_turned, whole = gather_all(packed, out_proj, normed)
+    out_turned = lax.all_gather(out_proj.T, "req", axis=0, tiled=True)
+    joined_piece, whole = gather_all(packed, normed)
     joined = jnp.dot(whole, joined_piece, preferred_element_type=jnp.float32)
     gates = joined[:, :first_end].astype(jnp.bfloat16)
     values = joined[:, first_end:second_end].astype(jnp.bfloat16)
@@ -258,9 +250,14 @@
         lower[None, :, :, None], running[:, :, None, :] - running[:, None, :, :], -jnp.inf
     )
     kernel = intersection[..., None] * jnp.exp(spread) * steps[:, None, :, :]
-    outputs = jnp.einsum("gtsh,gshp->gthp", kernel, vals_f, precision=HIGHEST)
+    outputs = jnp.einsum(
+        "gtsh,gshp->gthp", kernel.astype(jnp.bfloat16), vals, preferred_element_type=jnp.float32
+    )
     carried = jnp.einsum(
-        "gtn,ghpn->gthp", reads_c.astype(jnp.float32), state_start, precision=HIGHEST
+        "gtn,ghpn->gthp",
+        reads_c,
+        state_start.astype(jnp.bfloat16),
+        preferred_element_type=jnp.float32,
     )
     outputs = outputs + jnp.exp(running)[..., None] * carried + skip_gain[:, None] * vals_f
     product = outputs.reshape(group_rows, inner_here) * jax.nn.silu(gates.astype(jnp.float32))
@@ -293,7 +290,10 @@
     reach = jnp.where(before[:, :, None], running_last[:, None, :] - running, -jnp.inf)
     weights_s = jnp.exp(reach) * steps
     gathered_state = jnp.einsum(
-        "gsh,gshp,gsn->ghpn", weights_s, vals_f, inputs_b.astype(jnp.float32), precision=HIGHEST
+        "gshp,gsn->ghpn",
+        (weights_s[..., None] * vals_f).astype(jnp.bfloat16),
+        inputs_b,
+        preferred_element_type=jnp.float32,
     )
     state_here = jnp.exp(running_last)[:, :, None, None] * state_start + gathered_state
     picks = accepted[:, None] + jnp.arange(edge_count, dtype=jnp.int32)[None, :]

time: 154 us -> 158 us (1.026)
  between operations: 0.86 us -> 14.4 us
  matrix products: 25.7 us -> 16.5 us
  local copies, waits for them, and re-layouts: 20.9 us -> 14.2 us
  Pallas kernels: 80.9 us -> 86.5 us
  waiting for transfers between devices: 3.53 us -> 8.1 us
  other arithmetic: 16.8 us -> 12.8 us
    dot_general x3, matrix products: 12.7 us -> 4.59 us  [the longest x1 2.72 us: local(): jnp.einsum('gtsh,gshp->gthp', kernel.astype(jnp.bfloat16), vals, preferre...]
    pallas_call x1, Pallas kernels: 80.9 us -> 86.5 us  [ring_gather(): pl.pallas_call(lambda *refs: ring_kernel(count, *refs), out_shape=(jax.Sh...]
    ppermute x4, waiting for transfers between devices: 3.53 us -> 7.41 us  [swap(): return lax.ppermute(array, 'mdl', [(0, 1), (1, 0)])]
    reshape x2, local copies, waits for them, and re-layouts: 6.85 us -> 3.93 us  [local(): outputs.reshape(group_rows, inner_here)]
    slice x2, local copies, waits for them, and re-layouts: 3.23 us -> 1.21 us  [local(): active[..., :inner_here].reshape(requests, span, heads_here, head_dim)]
  transfers between devices with their start and end apart: 4 -> 5, of which waited for: 1 -> 2; matrix products, arithmetic and copies ran while one was open for 11% -> 25% of each run, Pallas kernels for 0% -> 55%
where the time goes in v3:
time: 158 us
  Pallas kernels  86.5 us (55%)
  matrix products  16.5 us (10%)
  between operations  14.4 us (9%)
  local copies, waits for them, and re-layouts  14.2 us (9%)
  other arithmetic  12.8 us (8%)
  waiting for transfers between devices  8.1 us (5%)
  starting transfers between devices  5.38 us (3%)
    pallas_call x1, Pallas kernels, ring_gather(): pl.pallas_call(lambda *refs: ring_kernel(count, *refs), out_shape=(jax.Sh...  86.5 us
    ppermute x4, waiting for transfers between devices, swap(): return lax.ppermute(array, 'mdl', [(0, 1), (1, 0)])  7.41 us
    dot_general x1, matrix products, local(): joined = jnp.dot(whole, joined_piece, preferred_element_type=jnp.float32)  7.29 us
    ppermute x4, starting transfers between devices, swap(): return lax.ppermute(array, 'mdl', [(0, 1), (1, 0)])  5.34 us
    dot_general x1, matrix products, local(): lax.dot_general(gated, out_turned, (((1,), (1,)), ((), ())), preferred_el...  4.18 us
    reshape x2, local copies, waits for them, and re-layouts, local(): outputs.reshape(group_rows, inner_here)  3.93 us
  transfers between devices with their start and end apart: 5, of which 2 were waited for; matrix products, arithmetic and copies ran while one was open for 25% of the time, Pallas kernels for 55%

profile of v3, /device:TPU:0, one launch (start us, length us, event | category | flops | bytes accessed | tf_op | source)
XLA Modules:
  0.0 157.8 jit_solution(10425212548540412069)
XLA Ops:
  7.2 0.0 copy-start.6
  7.2 0.0 all-gather.2.cloned.1.call-start
  7.2 0.7 all-gather.2.cloned.1.call-update
  7.9 0.8 copy.30
  8.7 1.2 fusion.21
  9.9 2.0 %fusion.31.refs_0_ = bf16[96,3456]{1,0:T(8,128)(2,1)} fusion(bf16[96,24]{1,0:T(8,128)(2,1)S(1)} %copy.30, bf16[96,256]{1,0:T(8,128)(2,1)} %param.22, bf16[96,1536]{1,0:T(8,128)(2,1)} %param.21, bf16[96,1536]{1,0:T(8,128)(2,1)} %param.20), kind=kLoop, calls=%fused_computation.57 | loop fusion | flops 4313088 | bytes 1307136 | tf_op jit(solution)/shard_map/concatenate | solution.py:217
  11.9 0.9 fusion.23.refs_1_
  12.8 86.5 %shard_map.193 = (bf16[16,96,3456]{2,1,0:T(8,128)(2,1)}, bf16[2,128,1536]{2,1,0:T(8,128)(2,1)}) custom-call(bf16[96,3456]{1,0:T(8,128)(2,1)} %fusion.31.refs_0_, bf16[128,1536]{1,0:T(8,128)(2,1)} %fusion.23.refs_1_), custom_call_target="tpu_custom_call" | custom-call | tf_op jit(solution)/shard_map/pallas_call | solution.py:140
  99.3 7.3 %convolution_convert_fusion = bf16[256,3456]{1,0:T(8,128)(2,1)S(1)} fusion(bf16[256,1536]{1,0:T(8,128)(2,1)} %bitcast.43, bf16[1536,3456]{1,0:T(8,128)(2,1)} %bitcast.42), kind=kOutput, calls=%fused_computation.1 | convolution fusion | flops 2718793728 | bytes 13172736 | tf_op jit(solution)/shard_map/dot_general | solution.py:220
  106.6 0.0 copy-start.11
  106.6 0.0 copy-start.14
  106.6 0.1 slice.81
  106.7 0.7 copy-done.11
  107.3 0.0 copy-done.14
  107.3 0.2 maximum_convert_fusion
  107.6 0.2 copy-done.5
  107.8 1.9 %copy.35 = bf16[2,131,1792]{2,0,1:T(2,128)(2,1)} copy(f32[2,131,1792]{2,1,0:T(8,128)S(1)} %maximum_convert_fusion) | data formatting | bytes 2817024 | tf_op jit(solution)/shard_map/convert_element_type | solution.py:227
  109.7 0.1 fusion.47
  109.8 0.1 reshape.242
  109.9 1.4 gather_fusion
  111.3 0.1 compare_and_fusion
  111.4 0.1 broadcast_select_fusion
  111.5 0.6 copy-done.7
  112.1 0.0 copy-start.8
  112.1 1.6 %collective-permute-start.3 = (bf16[1,3,1536]{2,1,0:T(4,128)(2,1)S(1)}, bf16[1,3,1536]{2,1,0:T(4,128)(2,1)}, u32[]{:S(2)}, u32[]{:S(2)}) collective-permute-start(bf16[1,3,1536]{2,1,0:T(4,128)(2,1)S(1)} %dynamic-slice_convert_fusion.1), channel_id=1, source_target_pairs={{0,1},{1,0},{2,3},{3,2},{4,5},{5,4},{6,7},{7,6},{8,9},{9,8},{10,11... | collective-permute-start | bytes 27656 | tf_op jit(solution)/shard_map/ppermute | solution.py:176
  113.8 0.1 slice_reduce_fusion.4
  113.9 1.2 multiply_convert_fusion.1
  115.1 0.0 slice-start
  115.1 0.0 copy-start.17
  115.1 0.0 copy-start.15
  115.1 0.0 copy-start
  115.1 0.1 slice.89
  115.2 1.2 copy.31
  116.3 0.1 copy.32
  116.4 0.1 iota_compare_fusion.3
  116.5 0.1 compare_select_fusion
  116.6 0.3 multiply_reduce_fusion.1
  116.9 0.1 exponential_multiply_fusion
  117.0 1.5 multiply_add_fusion
  118.5 0.9 dynamic-slice_convert_fusion
  119.5 0.5 collective-permute-start.2
  120.0 0.2 fusion.36
  120.1 0.0 copy-start.4
  120.1 0.0 copy-start.19
  120.2 0.4 fusion.27
  120.5 0.7 copy-done.4
  121.3 2.7 %fusion.5 = f32[2,128,24,64]{1,3,2,0:T(8,128)} fusion(bf16[2,128,24,64]{1,3,2,0:T(8,128)(2,1)S(1)} %bitcast.39, f32[2,128,24,64]{1,3,2,0:T(8,128)S(1)} %fusion.27, f32[2,128,24]{1,2,0:T(8,128)S(1)} %compare_select_fusion, f32[2,128,24]{1,2,0:T(8,128)S(1)} %get-tuple-element.21, f32[2,128,128]{2,1,0:T(8,128)S(1)} %fusion.36, ...), kind=kOutput, calls=%fused_computation.18 | convolution fusion | flops 106561536 | bytes 4153440 | tf_op jit(solution)/shard_map/gtsh,gshp->gthp/dot_general | solution.py:253
  124.0 2.2 %copy.38 = f32[2,128,24,64]{3,2,1,0:T(8,128)S(1)} copy(f32[2,128,24,64]{1,3,2,0:T(8,128)} %fusion.5) | data formatting | bytes 3145728 | tf_op jit(solution)/shard_map/reshape | solution.py:263
  126.3 1.7 %reshape.251 = f32[256,1536]{1,0:T(8,128)} reshape(f32[2,128,24,64]{3,2,1,0:T(8,128)S(1)} %copy.38) | data formatting | bytes 3145728 | tf_op jit(solution)/shard_map/reshape | solution.py:263
  128.0 2.3 %multiply_reduce_fusion = f32[256]{0:T(256)S(1)} fusion(f32[256,1536]{1,0:T(8,128)} %reshape.251, bf16[256,3456]{1,0:T(8,128)(2,1)} %copy-done.5), kind=kLoop, calls=%fused_computation.27 | loop fusion | flops 3145472 | bytes 2360320 | tf_op jit(solution)/shard_map/reduce_sum | solution.py:264
  130.2 1.6 %collective-permute-start.1 = (f32[256]{0:T(256)S(1)}, f32[256]{0:T(256)S(1)}, u32[]{:S(2)}, u32[]{:S(2)}) collective-permute-start(f32[256]{0:T(256)S(1)} %multiply_reduce_fusion), channel_id=1, source_target_pairs={{0,1},{1,0},{2,3},{3,2},{4,5},{5,4},{6,7},{7,6},{8,9},{9,8},{10,11... | collective-permute-start | bytes 3080 | tf_op jit(solution)/shard_map/ppermute | solution.py:176
  131.9 0.7 dynamic_slice.30
  132.5 0.7 compare_convert_fusion.1
  133.2 0.6 collective-permute-done.1
  133.9 0.6 dynamic_slice.29
  134.5 0.0 collective-permute-done.3
  134.5 0.7 fusion.40
  135.2 0.6 pad_maximum_fusion.1
  135.8 4.2 %convolution_convert_fusion.1 = bf16[256,1536]{1,0:T(8,128)(2,1)S(1)} fusion(bf16[1536,1536]{1,0:T(8,128)(2,1)} %all-gather.2.cloned.1.call-done, f32[1536]{0:T(1024)} %param.29, f32[256,1536]{1,0:T(8,128)S(1)} %copy-done.1, bf16[256,3456]{1,0:T(8,128)(2,1)} %copy-done.5), kind=kOutput, calls=%fused_computation.3 | convolution fusion | flops 1211498496 | bytes 7872512 | tf_op jit(solution)/shard_map/dot_general | solution.py:269
  140.1 1.6 %collective-permute-start = (bf16[128,1536]{1,0:T(8,128)(2,1)S(1)}, bf16[128,1536]{1,0:T(8,128)(2,1)S(1)}, u32[]{:S(2)}, u32[]{:S(2)}) collective-permute-start(bf16[128,1536]{1,0:T(8,128)(2,1)S(1)} %constant_dynamic-slice_fusion), channel_id=1, source_target_pairs={{0,1},{1,0},{2,3},{3,2},{4,5},{5,4},{6,7},{7,6},{8,9},{9,8},{10,11... | collective-permute-start | bytes 1179656 | tf_op jit(solution)/shard_map/ppermute | solution.py:176
  141.7 0.2 convert_select_fusion.1
  141.9 1.3 pad_maximum_fusion
  143.2 6.8 %collective-permute-done = bf16[128,1536]{1,0:T(8,128)(2,1)S(1)} collective-permute-done((bf16[128,1536]{1,0:T(8,128)(2,1)S(1)}, bf16[128,1536]{1,0:T(8,128)(2,1)S(1)}, u32[]{:S(2)}, u32[]{:S(2)}) %collective-permute-start) | collective-permute-done | bytes 393248 | tf_op jit(solution)/shard_map/ppermute | solution.py:176
  150.0 1.0 multiply_convert_fusion.7
  (48 shorter events, 0.3 us)
Async XLA Ops:
  7.2 4.7 %copy-start.6 = (bf16[128,1536]{1,0:T(8,128)(2,1)S(1)}, bf16[128,1536]{1,0:T(8,128)(2,1)}, u32[]{:S(2)}) copy-start(bf16[128,1536]{1,0:T(8,128)(2,1)} %param.18) | copy-start | bytes 1179652
  7.2 4.7 %copy-start.12 = (f32[1536]{0:T(1024)S(1)}, f32[1536]{0:T(1024)}, u32[]{:S(2)}) copy-start(f32[1536]{0:T(1024)} %param.19) | copy-start | bytes 18436
  7.2 128.7 %all-gather.2.cloned.1.call-start = ((), (), s32[]{:S(2)}) async-start(), calls=%async_computation | async-start | bytes 5013504 | tf_op jit(solution)/shard_map/all_gather | solution.py:218
  106.6 1.2 copy-start.5
  106.6 0.7 copy-start.11
  106.6 0.8 copy-start.14
  107.8 1.9 %copy-start.18 = (s32[2]{0:T(128)S(1)}, s32[2]{0:T(128)}, u32[]{:S(2)}) copy-start(s32[2]{0:T(128)} %param.35) | copy-start | bytes 28
  107.8 6.0 %copy-start.10 = (f32[5,1536]{1,0:T(8,128)S(1)}, f32[5,1536]{1,0:T(8,128)}, u32[]{:S(2)}) copy-start(f32[5,1536]{1,0:T(8,128)} %param.24) | copy-start | bytes 92164
  107.8 6.0 %copy-start.13 = (f32[5,256]{1,0:T(8,128)S(1)}, f32[5,256]{1,0:T(8,128)}, u32[]{:S(2)}) copy-start(f32[5,256]{1,0:T(8,128)} %param.25) | copy-start | bytes 15364
  111.5 0.6 copy-start.7
  112.1 1.8 %copy-start.8 = (bf16[2,3,1536]{2,1,0:T(4,128)(2,1)}, bf16[2,3,1536]{2,1,0:T(4,128)(2,1)S(1)}, u32[]{:S(2)}) copy-start(bf16[2,3,1536]{2,1,0:T(4,128)(2,1)S(1)} %slice.94) | copy-start | bytes 55300
  112.1 22.4 %collective-permute-start.3 = (bf16[1,3,1536]{2,1,0:T(4,128)(2,1)S(1)}, bf16[1,3,1536]{2,1,0:T(4,128)(2,1)}, u32[]{:S(2)}, u32[]{:S(2)}) collective-permute-start(bf16[1,3,1536]{2,1,0:T(4,128)(2,1)S(1)} %dynamic-slice_convert_fusion.1), channel_id=1, source_target_pairs={{0,1},{1,0},{2,3},{3,2},{4,5},{5,4},{6,7},{7,6},{8,9},{9,8},{10,11... | collective-permute-start | bytes 27656 | tf_op jit(solution)/shard_map/ppermute | solution.py:176
  115.1 1.3 slice-start
  115.1 1.3 copy-start.17
  115.1 1.4 copy-start.15
  115.1 1.9 %copy-start = (f32[2,24,64,128]{3,2,1,0:T(8,128)S(1)}, f32[2,24,64,128]{3,2,1,0:T(8,128)}, u32[]{:S(2)}) copy-start(f32[2,24,64,128]{3,2,1,0:T(8,128)} %param.31) | copy-start | bytes 4718596
  118.5 2.0 %copy-start.2 = (f32[2,24,64,128]{3,2,1,0:T(8,128)}, f32[2,24,64,128]{3,2,1,0:T(8,128)S(1)}, u32[]{:S(2)}) copy-start(f32[2,24,64,128]{3,2,1,0:T(8,128)S(1)} %multiply_add_fusion) | copy-start | bytes 4718596
  119.5 22.2 %collective-permute-start.2 = (bf16[1,24,64,128]{3,2,1,0:T(8,128)(2,1)}, bf16[1,24,64,128]{3,2,1,0:T(8,128)(2,1)S(1)}, u32[]{:S(2)}, u32[]{:S(2)}) collective-permute-start(bf16[1,24,64,128]{3,2,1,0:T(8,128)(2,1)} %dynamic-slice_convert_fusion), channel_id=1, source_target_pairs={{0,1},{1,0},{2,3},{3,2},{4,5},{5,4},{6,7},{7,6},{8,9},{9,8},{10,11... | collective-permute-start | bytes 1179656 | tf_op jit(solution)/shard_map/ppermute | solution.py:176
  120.1 1.1 copy-start.4
  120.1 1.1 copy-start.19
  127.9 3.9 %copy-start.20 = (s32[2]{0:T(128)S(1)}, s32[2]{0:T(128)}, u32[]{:S(2)}) copy-start(s32[2]{0:T(128)} %param.34) | copy-start | bytes 28
  127.9 4.6 %slice-start.1 = ((bf16[2,3,1792]{2,1,0:T(4,128)(2,1)}), bf16[2,3,256]{2,1,0:T(4,128)(2,1)S(1)}, s32[]{:S(2)}) async-start(bf16[2,3,1792]{2,1,0:T(4,128)(2,1)} %copy-done.7), calls=%async_computation.2 | async-start | bytes 8192 | tf_op jit(solution)/shard_map/slice | solution.py:336
  127.9 6.5 %copy-start.9 = (bf16[2,3,1536]{2,1,0:T(4,128)(2,1)S(1)}, bf16[2,3,1536]{2,1,0:T(4,128)(2,1)}, u32[]{:S(2)}) copy-start(bf16[2,3,1536]{2,1,0:T(4,128)(2,1)} %copy-done.8) | copy-start | bytes 55300
  127.9 7.9 %copy-start.1 = (f32[256,1536]{1,0:T(8,128)S(1)}, f32[256,1536]{1,0:T(8,128)}, u32[]{:S(2)}) copy-start(f32[256,1536]{1,0:T(8,128)} %reshape.251) | copy-start | bytes 4718596
  130.2 3.6 %collective-permute-start.1 = (f32[256]{0:T(256)S(1)}, f32[256]{0:T(256)S(1)}, u32[]{:S(2)}, u32[]{:S(2)}) collective-permute-start(f32[256]{0:T(256)S(1)} %multiply_reduce_fusion), channel_id=1, source_target_pairs={{0,1},{1,0},{2,3},{3,2},{4,5},{5,4},{6,7},{7,6},{8,9},{9,8},{10,11... | collective-permute-start | bytes 3080 | tf_op jit(solution)/shard_map/ppermute | solution.py:176
  135.8 5.9 %copy-start.3 = (f32[2,24,64,128]{3,2,1,0:T(8,128)S(1)}, f32[2,24,64,128]{3,2,1,0:T(8,128)}, u32[]{:S(2)}) copy-start(f32[2,24,64,128]{3,2,1,0:T(8,128)} %copy-done.2) | copy-start | bytes 4718596
  140.1 9.9 %collective-permute-start = (bf16[128,1536]{1,0:T(8,128)(2,1)S(1)}, bf16[128,1536]{1,0:T(8,128)(2,1)S(1)}, u32[]{:S(2)}, u32[]{:S(2)}) collective-permute-start(bf16[128,1536]{1,0:T(8,128)(2,1)S(1)} %constant_dynamic-slice_fusion), channel_id=1, source_target_pairs={{0,1},{1,0},{2,3},{3,2},{4,5},{5,4},{6,7},{7,6},{8,9},{9,8},{10,11... | collective-permute-start | bytes 1179656 | tf_op jit(solution)/shard_map/ppermute | solution.py:176
  141.9 8.1 %copy-start.16 = (f32[128]{0:T(128)S(1)}, f32[128]{0:T(128)}, u32[]{:S(2)}) copy-start(f32[128]{0:T(128)} %dynamic_slice.29) | copy-start | bytes 1540
Sparse Core Ops, SparseCore 0:
  10.3 76.4 all-gather.1

commit v4 on v2

--- a/solution.py
+++ b/solution.py
@@ -258,9 +258,14 @@
         lower[None, :, :, None], running[:, :, None, :] - running[:, None, :, :], -jnp.inf
     )
     kernel = intersection[..., None] * jnp.exp(spread) * steps[:, None, :, :]
-    outputs = jnp.einsum("gtsh,gshp->gthp", kernel, vals_f, precision=HIGHEST)
+    outputs = jnp.einsum(
+        "gtsh,gshp->gthp", kernel.astype(jnp.bfloat16), vals, preferred_element_type=jnp.float32
+    )
     carried = jnp.einsum(
-        "gtn,ghpn->gthp", reads_c.astype(jnp.float32), state_start, precision=HIGHEST
+        "gtn,ghpn->gthp",
+        reads_c,
+        state_start.astype(jnp.bfloat16),
+        preferred_element_type=jnp.float32,
     )
     outputs = outputs + jnp.exp(running)[..., None] * carried + skip_gain[:, None] * vals_f
     product = outputs.reshape(group_rows, inner_here) * jax.nn.silu(gates.astype(jnp.float32))
@@ -293,7 +298,10 @@
     reach = jnp.where(before[:, :, None], running_last[:, None, :] - running, -jnp.inf)
     weights_s = jnp.exp(reach) * steps
     gathered_state = jnp.einsum(
-        "gsh,gshp,gsn->ghpn", weights_s, vals_f, inputs_b.astype(jnp.float32), precision=HIGHEST
+        "gshp,gsn->ghpn",
+        (weights_s[..., None] * vals_f).astype(jnp.bfloat16),
+        inputs_b,
+        preferred_element_type=jnp.float32,
     )
     state_here = jnp.exp(running_last)[:, :, None, None] * state_start + gathered_state
     picks = accepted[:, None] + jnp.arange(edge_count, dtype=jnp.int32)[None, :]

time: 154 us -> 151 us (0.981)
  matrix products: 25.7 us -> 22.5 us
    dot_general x3, matrix products: 12.7 us -> 9.5 us  [the longest x1 4.45 us: local(): jnp.einsum('gtsh,gshp->gthp', kernel.astype(jnp.bfloat16), vals, preferre...]
  transfers between devices with their start and end apart: 4 -> 4, of which waited for: 1 -> 1; matrix products, arithmetic and copies ran while one was open for 11% -> 10% of each run, Pallas kernels for 0% -> 0%
where the time goes in v4:
time: 151 us; the launch traced here: 150 us
  Pallas kernels  80.9 us (54%)
  matrix products  22.5 us (15%)
  local copies, waits for them, and re-layouts  20.9 us (14%)
  other arithmetic  16.8 us (11%)
  starting transfers between devices  4.2 us (3%)
  waiting for transfers between devices  3.53 us (2%)
    pallas_call x1, Pallas kernels, ring_gather(): pl.pallas_call(lambda *refs: ring_kernel(count, *refs), out_shape=(jax.Sh...  80.9 us
    dot_general x1, matrix products, local(): joined = jnp.dot(whole, joined_piece, preferred_element_type=jnp.float32)  7.29 us
    reshape x2, local copies, waits for them, and re-layouts, local(): outputs.reshape(group_rows, inner_here)  6.85 us
    dot_general x1, matrix products, local(): lax.dot_general(gated, out_turned, (((1,), (1,)), ((), ())), preferred_el...  4.64 us
    dot_general x1, matrix products, local(): jnp.einsum('gtsh,gshp->gthp', kernel.astype(jnp.bfloat16), vals, preferre...  4.45 us
    ppermute x4, starting transfers between devices, swap(): return lax.ppermute(array, 'mdl', [(0, 1), (1, 0)])  4.2 us
    ppermute x4, waiting for transfers between devices, swap(): return lax.ppermute(array, 'mdl', [(0, 1), (1, 0)])  3.53 us
    slice x2, local copies, waits for them, and re-layouts, local(): active[..., :inner_here].reshape(requests, span, heads_here, head_dim)  3.23 us
  transfers between devices with their start and end apart: 4, of which 1 were waited for; matrix products, arithmetic and copies ran while one was open for 10% of the time, Pallas kernels for 0%

profile of v4, /device:TPU:0, one launch (start us, length us, event | category | flops | bytes accessed | tf_op | source)
XLA Modules:
  0.0 149.7 jit_solution(2084904335841153122)
XLA Ops:
  0.6 0.8 copy.30
  1.4 1.2 fusion.21
  2.6 1.9 %fusion.23.refs_2_ = bf16[128,1536]{1,0:T(8,128)(2,1)} fusion(bf16[128,1536]{1,0:T(8,128)(2,1)} %param.18, f32[1536]{0:T(1024)} %param.19, f32[128]{0:T(128)S(1)} %add_rsqrt_fusion.1), kind=kLoop, calls=%fused_computation.48 | loop fusion | flops 786432 | bytes 793088 | tf_op jit(solution)/shard_map/convert_element_type | solution.py:220
  4.5 2.0 %fusion.31.refs_0_ = bf16[96,3456]{1,0:T(8,128)(2,1)} fusion(bf16[96,24]{1,0:T(8,128)(2,1)S(1)} %copy.30, bf16[96,256]{1,0:T(8,128)(2,1)} %param.22, bf16[96,1536]{1,0:T(8,128)(2,1)} %param.21, bf16[96,1536]{1,0:T(8,128)(2,1)} %param.20), kind=kLoop, calls=%fused_computation.57 | loop fusion | flops 4313088 | bytes 1307136 | tf_op jit(solution)/shard_map/concatenate | solution.py:226
  6.5 80.9 %shard_map.193 = (bf16[16,96,3456]{2,1,0:T(8,128)(2,1)}, bf16[16,96,1536]{2,1,0:T(8,128)(2,1)}, bf16[2,128,1536]{2,1,0:T(8,128)(2,1)}) custom-call(bf16[96,3456]{1,0:T(8,128)(2,1)} %fusion.31.refs_0_, bf16[96,1536]{1,0:T(8,128)(2,1)} %bitcast.41, bf16[128,1536]{1,0:T(8,128)(2,1)} %fusion.23.refs_2_), custom_call_target="tpu_custom_call" | custom-call | tf_op jit(solution)/shard_map/pallas_call | solution.py:146
  87.3 7.3 %convolution_convert_fusion = bf16[256,3456]{1,0:T(8,128)(2,1)S(1)} fusion(bf16[256,1536]{1,0:T(8,128)(2,1)} %bitcast.45, bf16[1536,3456]{1,0:T(8,128)(2,1)} %bitcast.43), kind=kOutput, calls=%fused_computation.1 | convolution fusion | flops 2718793728 | bytes 13172736 | tf_op jit(solution)/shard_map/dot_general | solution.py:228
  94.6 0.0 copy-start.11
  94.7 0.0 copy-start.9
  94.7 0.0 copy-start.8
  94.7 0.0 copy-start.10
  94.7 0.1 slice.81
  94.8 0.6 slice.92
  95.4 0.1 copy-done.9
  95.5 0.1 copy-done.8
  95.6 0.1 slice_reduce_fusion.4
  95.7 0.2 copy-done.4
  95.9 0.2 maximum_convert_fusion
  96.1 1.2 multiply_convert_fusion.1
  97.3 0.0 copy-start
  97.3 0.9 slice.89
  98.2 0.2 copy-done.3
  98.5 0.8 fusion.36
  99.3 0.6 iota_compare_fusion.1
  99.9 2.3 %copy.31 = bf16[2,128,1536]{1,2,0:T(8,128)(2,1)} copy(bf16[2,128,1536]{2,1,0:T(8,128)(2,1)} %slice.89) | data formatting | bytes 1572864 | tf_op jit(solution)/shard_map/slice | solution.py:243
  102.2 2.4 %fusion.27 = f32[2,128,24,64]{1,3,2,0:T(8,128)} fusion(f32[2,24,64,128]{3,2,1,0:T(8,128)S(1)} %copy-done, bf16[2,128,1792]{2,1,0:T(8,128)(2,1)} %copy-done.3), kind=kOutput, calls=%fused_computation.53 | convolution fusion | flops 101056512 | bytes 3211264 | tf_op jit(solution)/shard_map/gtn,ghpn->gthp/dot_general | solution.py:264
  104.6 0.9 copy.32
  105.5 0.7 broadcast_add_fusion
  106.1 0.1 iota_compare_fusion.3
  106.2 0.1 compare_select_fusion
  106.3 0.3 multiply_reduce_fusion.1
  106.6 0.7 exponential_multiply_fusion
  107.4 4.4 %fusion.5 = f32[2,128,24,64]{1,3,2,0:T(8,128)} fusion(bf16[2,128,24,64]{1,3,2,0:T(8,128)(2,1)} %bitcast.39, f32[2,128,24,64]{1,3,2,0:T(8,128)} %fusion.27, f32[2,128,24]{1,2,0:T(8,128)S(1)} %compare_select_fusion, f32[2,128,24]{1,2,0:T(8,128)S(1)} %get-tuple-element.23, f32[2,128,128]{2,1,0:T(8,128)} %fusion.36, pred[128,128]{1,0:T(8,128)(4,1)} %iota_compare_fusion.1, ...), kind=kOutput, calls=%fused_computation.18 | convolution fusion | flops 106561536 | bytes 4153440 | tf_op jit(solution)/shard_map/gtsh,gshp->gthp/dot_general | solution.py:261
  111.8 3.3 %copy.38 = f32[2,128,24,64]{3,2,1,0:T(8,128)} copy(f32[2,128,24,64]{1,3,2,0:T(8,128)} %fusion.5) | data formatting | bytes 3145728 | tf_op jit(solution)/shard_map/reshape | solution.py:271
  115.1 3.6 %reshape.255 = f32[256,1536]{1,0:T(8,128)} reshape(f32[2,128,24,64]{3,2,1,0:T(8,128)} %copy.38) | data formatting | bytes 3145728 | tf_op jit(solution)/shard_map/reshape | solution.py:271
  118.7 4.6 %convolution_convert_fusion.1 = bf16[256,1536]{1,0:T(8,128)(2,1)S(1)} fusion(bf16[1536,1536]{1,0:T(8,128)(2,1)} %bitcast.44, f32[1536]{0:T(1024)S(1)} %copy-done.13, f32[256,1536]{1,0:T(8,128)} %reshape.255, bf16[256,3456]{1,0:T(8,128)(2,1)} %copy-done.4), kind=kOutput, calls=%fused_computation.3 | convolution fusion | flops 1211498496 | bytes 7870464 | tf_op jit(solution)/shard_map/dot_general | solution.py:277
  123.3 0.0 copy-start.7
  123.3 0.8 constant_dynamic-slice_fusion
  124.2 1.5 %collective-permute-start = (bf16[128,1536]{1,0:T(8,128)(2,1)}, bf16[128,1536]{1,0:T(8,128)(2,1)}, u32[]{:S(2)}, u32[]{:S(2)}) collective-permute-start(bf16[128,1536]{1,0:T(8,128)(2,1)} %constant_dynamic-slice_fusion), channel_id=1, source_target_pairs={{0,1},{1,0},{2,3},{3,2},{4,5},{5,4},{6,7},{7,6},{8,9},{9,8},{10,11... | collective-permute-start | bytes 1179656 | tf_op jit(solution)/shard_map/ppermute | solution.py:185
  125.7 1.7 %multiply_reduce_fusion = f32[256]{0:T(256)S(1)} fusion(f32[256,1536]{1,0:T(8,128)S(1)} %copy-done.1, bf16[256,3456]{1,0:T(8,128)(2,1)} %copy-done.4), kind=kLoop, calls=%fused_computation.27 | loop fusion | flops 3145472 | bytes 2360320 | tf_op jit(solution)/shard_map/reduce_sum | solution.py:272
  127.4 0.6 collective-permute-start.1
  128.0 0.6 exp.41
  128.6 2.7 %multiply_add_fusion = f32[2,24,64,128]{3,2,1,0:T(8,128)} fusion(f32[2,24,64,128]{3,2,1,0:T(8,128)S(1)} %copy-done, bf16[2,128,24,64]{1,3,2,0:T(8,128)(2,1)} %bitcast.40, f32[2,128,24]{1,2,0:T(8,128)S(1)} %copy-done.7, f32[2,24]{1,0:T(2,128)} %exp.41, bf16[2,128,1792]{2,1,0:T(8,128)(2,1)} %copy-done.3), kind=kOutput, calls=%fused_computation.26 | convolution fusion | flops 102629376 | bytes 4023296 | tf_op jit(solution)/shard_map/gshp,gsn->ghpn/dot_general | solution.py:300
  131.3 2.0 %dynamic-slice_convert_fusion = bf16[1,24,64,128]{3,2,1,0:T(8,128)(2,1)} fusion(f32[2,24,64,128]{3,2,1,0:T(8,128)} %multiply_add_fusion, s32[]{:T(128)S(6)} %select_n.84), kind=kLoop, calls=%fused_computation.49 | loop fusion | bytes 786436 | tf_op jit(solution)/shard_map/convert_element_type | solution.py:313
  133.2 1.5 %collective-permute-start.2 = (bf16[1,24,64,128]{3,2,1,0:T(8,128)(2,1)}, bf16[1,24,64,128]{3,2,1,0:T(8,128)(2,1)}, u32[]{:S(2)}, u32[]{:S(2)}) collective-permute-start(bf16[1,24,64,128]{3,2,1,0:T(8,128)(2,1)} %dynamic-slice_convert_fusion), channel_id=1, source_target_pairs={{0,1},{1,0},{2,3},{3,2},{4,5},{5,4},{6,7},{7,6},{8,9},{9,8},{10,11... | collective-permute-start | bytes 1179656 | tf_op jit(solution)/shard_map/ppermute | solution.py:185
  134.7 1.9 %copy.35 = bf16[2,131,1792]{2,0,1:T(2,128)(2,1)} copy(f32[2,131,1792]{2,1,0:T(8,128)S(1)} %maximum_convert_fusion) | data formatting | bytes 2817024 | tf_op jit(solution)/shard_map/convert_element_type | solution.py:235
  136.7 0.1 fusion.47
  136.7 0.1 compare_and_fusion
  136.8 0.1 reshape.246
  136.9 1.4 gather_fusion
  138.3 0.1 broadcast_select_fusion
  138.5 0.6 collective-permute-start.3
  139.0 0.6 dynamic_slice.30
  139.6 0.6 compare_convert_fusion.1
  140.3 0.0 collective-permute-done.1
  140.3 0.6 add_rsqrt_fusion
  140.9 0.1 dynamic_slice.29
  141.0 3.5 %collective-permute-done.3 = bf16[1,3,1536]{2,1,0:T(4,128)(2,1)S(1)} collective-permute-done((bf16[1,3,1536]{2,1,0:T(4,128)(2,1)S(1)}, bf16[1,3,1536]{2,1,0:T(4,128)(2,1)S(1)}, u32[]{:S(2)}, u32[]{:S(2)}) %collective-permute-start.3) | collective-permute-done | bytes 9248 | tf_op jit(solution)/shard_map/ppermute | solution.py:185
  144.5 0.6 pad_maximum_fusion.1
  145.2 0.0 collective-permute-done.2
  145.2 1.2 convert_select_fusion.1
  146.4 1.2 pad_maximum_fusion
  147.6 0.0 collective-permute-done
  147.6 0.2 copy-done.6
  147.8 2.0 %multiply_convert_fusion.7 = bf16[128,1536]{1,0:T(8,128)(2,1)} fusion(bf16[128,1536]{1,0:T(8,128)(2,1)} %collective-permute-done, f32[128]{0:T(128)S(1)} %compare_convert_fusion.1, f32[128]{0:T(128)S(1)} %dynamic_slice.29, bf16[256,1536]{1,0:T(8,128)(2,1)S(1)} %copy-done.6, s32[]{:T(128)S(6)} %select_n.79), kind=kLoop, calls=%fused_computation.51 | loop fusion | flops 1179648 | bytes 1180676 | tf_op jit(solution)/shard_map/convert_element_type | solution.py:293
  (35 shorter events, 0.2 us)
Async XLA Ops:
  94.6 1.2 copy-start.4
  94.6 0.7 copy-start.11
  94.7 0.8 copy-start.9
  94.7 0.9 copy-start.8
  94.7 0.9 copy-start.10
  97.3 1.2 copy-start.3
  97.3 4.9 %copy-start = (f32[2,24,64,128]{3,2,1,0:T(8,128)S(1)}, f32[2,24,64,128]{3,2,1,0:T(8,128)}, u32[]{:S(2)}) copy-start(f32[2,24,64,128]{3,2,1,0:T(8,128)} %param.31) | copy-start | bytes 4718596
  102.2 4.0 %copy-start.14 = (f32[24]{0:T(128)S(1)}, f32[24]{0:T(128)}, u32[]{:S(2)}) copy-start(f32[24]{0:T(128)} %param.27) | copy-start | bytes 292
  102.2 4.0 %copy-start.12 = (f32[24]{0:T(128)S(1)}, f32[24]{0:T(128)}, u32[]{:S(2)}) copy-start(f32[24]{0:T(128)} %param.26) | copy-start | bytes 292
  115.1 3.6 %copy-start.13 = (f32[1536]{0:T(1024)S(1)}, f32[1536]{0:T(1024)}, u32[]{:S(2)}) copy-start(f32[1536]{0:T(1024)} %param.29) | copy-start | bytes 18436
  118.7 7.1 %copy-start.1 = (f32[256,1536]{1,0:T(8,128)S(1)}, f32[256,1536]{1,0:T(8,128)}, u32[]{:S(2)}) copy-start(f32[256,1536]{1,0:T(8,128)} %reshape.255) | copy-start | bytes 4718596
  123.3 4.1 %copy-start.5 = (bf16[256,1536]{1,0:T(8,128)(2,1)}, bf16[256,1536]{1,0:T(8,128)(2,1)S(1)}, u32[]{:S(2)}) copy-start(bf16[256,1536]{1,0:T(8,128)(2,1)S(1)} %convolution_convert_fusion.1) | copy-start | bytes 2359300
  123.3 5.3 %copy-start.7 = (f32[2,128,24]{1,2,0:T(8,128)S(1)}, f32[2,128,24]{1,2,0:T(8,128)}, u32[]{:S(2)}) copy-start(f32[2,128,24]{1,2,0:T(8,128)} %get-tuple-element.18) | copy-start | bytes 73732
  124.2 23.4 %collective-permute-start = (bf16[128,1536]{1,0:T(8,128)(2,1)}, bf16[128,1536]{1,0:T(8,128)(2,1)}, u32[]{:S(2)}, u32[]{:S(2)}) collective-permute-start(bf16[128,1536]{1,0:T(8,128)(2,1)} %constant_dynamic-slice_fusion), channel_id=1, source_target_pairs={{0,1},{1,0},{2,3},{3,2},{4,5},{5,4},{6,7},{7,6},{8,9},{9,8},{10,11... | collective-permute-start | bytes 1179656 | tf_op jit(solution)/shard_map/ppermute | solution.py:185
  127.4 12.9 %collective-permute-start.1 = (f32[256]{0:T(256)S(1)}, f32[256]{0:T(256)}, u32[]{:S(2)}, u32[]{:S(2)}) collective-permute-start(f32[256]{0:T(256)S(1)} %multiply_reduce_fusion), channel_id=1, source_target_pairs={{0,1},{1,0},{2,3},{3,2},{4,5},{5,4},{6,7},{7,6},{8,9},{9,8},{10,11... | collective-permute-start | bytes 3080 | tf_op jit(solution)/shard_map/ppermute | solution.py:185
  133.2 3.4 %copy-start.15 = (s32[2]{0:T(128)S(1)}, s32[2]{0:T(128)}, u32[]{:S(2)}) copy-start(s32[2]{0:T(128)} %param.35) | copy-start | bytes 28
  133.2 5.8 %copy-start.16 = (s32[2]{0:T(128)S(1)}, s32[2]{0:T(128)}, u32[]{:S(2)}) copy-start(s32[2]{0:T(128)} %param.34) | copy-start | bytes 28
  133.2 11.9 %copy-start.2 = (f32[2,24,64,128]{3,2,1,0:T(8,128)S(1)}, f32[2,24,64,128]{3,2,1,0:T(8,128)}, u32[]{:S(2)}) copy-start(f32[2,24,64,128]{3,2,1,0:T(8,128)} %multiply_add_fusion) | copy-start | bytes 4718596
  133.2 11.9 %collective-permute-start.2 = (bf16[1,24,64,128]{3,2,1,0:T(8,128)(2,1)}, bf16[1,24,64,128]{3,2,1,0:T(8,128)(2,1)}, u32[]{:S(2)}, u32[]{:S(2)}) collective-permute-start(bf16[1,24,64,128]{3,2,1,0:T(8,128)(2,1)} %dynamic-slice_convert_fusion), channel_id=1, source_target_pairs={{0,1},{1,0},{2,3},{3,2},{4,5},{5,4},{6,7},{7,6},{8,9},{9,8},{10,11... | collective-permute-start | bytes 1179656 | tf_op jit(solution)/shard_map/ppermute | solution.py:185
  138.5 6.1 %collective-permute-start.3 = (bf16[1,3,1536]{2,1,0:T(4,128)(2,1)S(1)}, bf16[1,3,1536]{2,1,0:T(4,128)(2,1)S(1)}, u32[]{:S(2)}, u32[]{:S(2)}) collective-permute-start(bf16[1,3,1536]{2,1,0:T(4,128)(2,1)S(1)} %dynamic-slice_convert_fusion.1), channel_id=1, source_target_pairs={{0,1},{1,0},{2,3},{3,2},{4,5},{5,4},{6,7},{7,6},{8,9},{9,8},{10,11... | collective-permute-start | bytes 27656 | tf_op jit(solution)/shard_map/ppermute | solution.py:185
  146.3 1.4 copy-start.6

commit v5 on v4

--- a/solution.py
+++ b/solution.py
@@ -268,9 +268,10 @@
         preferred_element_type=jnp.float32,
     )
     outputs = outputs + jnp.exp(running)[..., None] * carried + skip_gain[:, None] * vals_f
-    product = outputs.reshape(group_rows, inner_here) * jax.nn.silu(gates.astype(jnp.float32))
-    squares = jnp.sum(product * product, -1)
-    gated = (product * output_gain).astype(jnp.bfloat16)
+    product = outputs * jax.nn.silu(gates.astype(jnp.float32).reshape(outputs.shape))
+    squares = jnp.sum(product * product, (2, 3)).reshape(group_rows)
+    gated = (product * output_gain.reshape(heads_here, head_dim)).astype(jnp.bfloat16)
+    gated = gated.reshape(group_rows, inner_here)
     paired = lax.axis_size("mdl") == 2
     total_squares = squares + swap(squares) if paired else lax.psum(squares, "mdl")
     scale = lax.rsqrt(total_squares / (inner_here * lax.axis_size("mdl")) + EPSILON)

time: 151 us -> 140 us (0.927)
  local copies, waits for them, and re-layouts: 20.9 us -> 14.4 us
  matrix products: 22.5 us -> 18.7 us
  other arithmetic: 16.8 us -> 15.1 us
    slice x2, local copies, waits for them, and re-layouts: 3.23 us -> 0.42 us  [local(): active[..., :inner_here].reshape(requests, span, heads_here, head_dim)]
    reshape x2, local copies, waits for them, and re-layouts: 6.85 us -> 4.47 us  [local(): gates.astype(jnp.float32).reshape(outputs.shape)]
    dot_general x1, matrix products: 4.45 us -> 2.66 us  [local(): jnp.einsum('gtsh,gshp->gthp', kernel.astype(jnp.bfloat16), vals, preferre...]
    reduce_sum x1 -> x0, other arithmetic: 1.7 us -> none  [local(): squares = jnp.sum(product * product, -1)]
  transfers between devices with their start and end apart: 4 -> 4, of which waited for: 1 -> 1; matrix products, arithmetic and copies ran while one was open for 10% -> 20% of each run, Pallas kernels for 0% -> 0%
where the time goes in v5:
time: 140 us; the launch traced here: 139 us
  Pallas kernels  80.9 us (58%)
  matrix products  18.7 us (13%)
  other arithmetic  15.1 us (11%)
  local copies, waits for them, and re-layouts  14.4 us (10%)
  waiting for transfers between devices  4.66 us (3%)
  starting transfers between devices  4.19 us (3%)
    pallas_call x1, Pallas kernels, ring_gather(): pl.pallas_call(lambda *refs: ring_kernel(count, *refs), out_shape=(jax.Sh...  80.9 us
    dot_general x1, matrix products, local(): joined = jnp.dot(whole, joined_piece, preferred_element_type=jnp.float32)  7.29 us
    ppermute x4, waiting for transfers between devices, swap(): return lax.ppermute(array, 'mdl', [(0, 1), (1, 0)])  4.66 us
    reshape x2, local copies, waits for them, and re-layouts, local(): gates.astype(jnp.float32).reshape(outputs.shape)  4.47 us
    ppermute x4, starting transfers between devices, swap(): return lax.ppermute(array, 'mdl', [(0, 1), (1, 0)])  4.19 us
    dot_general x1, matrix products, local(): lax.dot_general(gated, out_turned, (((1,), (1,)), ((), ())), preferred_el...  3.89 us
  transfers between devices with their start and end apart: 4, of which 1 were waited for; matrix products, arithmetic and copies ran while one was open for 20% of the time, Pallas kernels for 0%

profile of v5, /device:TPU:0, one launch (start us, length us, event | category | flops | bytes accessed | tf_op | source)
XLA Modules:
  0.0 139.0 jit_solution(6621452397943318541)
XLA Ops:
  0.6 0.7 fusion.44
  1.4 0.7 compare_and_fusion
  2.1 0.8 copy.31
  2.9 1.2 fusion.18
  4.1 1.9 %fusion.20.refs_2_ = bf16[128,1536]{1,0:T(8,128)(2,1)} fusion(bf16[128,1536]{1,0:T(8,128)(2,1)} %param.18, f32[1536]{0:T(1024)} %param.19, f32[128]{0:T(128)S(1)} %add_rsqrt_fusion.1), kind=kLoop, calls=%fused_computation.43 | loop fusion | flops 786432 | bytes 793088 | tf_op jit(solution)/shard_map/convert_element_type | solution.py:220
  6.0 2.0 %fusion.28.refs_0_ = bf16[96,3456]{1,0:T(8,128)(2,1)} fusion(bf16[96,24]{1,0:T(8,128)(2,1)S(1)} %copy.31, bf16[96,256]{1,0:T(8,128)(2,1)} %param.22, bf16[96,1536]{1,0:T(8,128)(2,1)} %param.21, bf16[96,1536]{1,0:T(8,128)(2,1)} %param.20), kind=kLoop, calls=%fused_computation.53 | loop fusion | flops 4313088 | bytes 1307136 | tf_op jit(solution)/shard_map/concatenate | solution.py:226
  7.9 80.9 %shard_map.193 = (bf16[16,96,3456]{2,1,0:T(8,128)(2,1)}, bf16[16,96,1536]{2,1,0:T(8,128)(2,1)}, bf16[2,128,1536]{2,1,0:T(8,128)(2,1)}) custom-call(bf16[96,3456]{1,0:T(8,128)(2,1)} %fusion.28.refs_0_, bf16[96,1536]{1,0:T(8,128)(2,1)} %bitcast.53, bf16[128,1536]{1,0:T(8,128)(2,1)} %fusion.20.refs_2_), custom_call_target="tpu_custom_call" | custom-call | tf_op jit(solution)/shard_map/pallas_call | solution.py:146
  88.8 7.3 %convolution_convert_fusion = bf16[256,3456]{1,0:T(8,128)(2,1)S(1)} fusion(bf16[256,1536]{1,0:T(8,128)(2,1)} %bitcast.57, bf16[1536,3456]{1,0:T(8,128)(2,1)} %bitcast.55), kind=kOutput, calls=%fused_computation.1 | convolution fusion | flops 2718793728 | bytes 13172736 | tf_op jit(solution)/shard_map/dot_general | solution.py:228
  96.1 0.0 copy-start.15
  96.1 0.0 copy-start.17
  96.1 0.1 slice.81
  96.2 0.7 copy-done.15
  96.9 0.0 copy-done.17
  96.9 0.2 maximum_convert_fusion
  97.1 0.2 copy-done.5
  97.3 1.0 copy.38
  98.3 0.1 reshape.260
  98.4 0.6 gather_fusion
  99.1 0.1 broadcast_select_fusion
  99.2 0.6 copy-done.9
  99.8 0.6 dynamic-slice_convert_fusion.1
  100.4 1.5 %collective-permute-start.3 = (bf16[1,3,1536]{2,1,0:T(4,128)(2,1)}, bf16[1,3,1536]{2,1,0:T(4,128)(2,1)}, u32[]{:S(2)}, u32[]{:S(2)}) collective-permute-start(bf16[1,3,1536]{2,1,0:T(4,128)(2,1)} %dynamic-slice_convert_fusion.1), channel_id=1, source_target_pairs={{0,1},{1,0},{2,3},{3,2},{4,5},{5,4},{6,7},{7,6},{8,9},{9,8},{10,11... | collective-permute-start | bytes 27656 | tf_op jit(solution)/shard_map/ppermute | solution.py:185
  101.9 0.1 slice_reduce_fusion.4
  102.1 1.2 multiply_convert_fusion.1
  103.2 0.0 slice-start
  103.3 0.0 copy-start.21
  103.3 0.0 copy-start.18
  103.3 0.1 slice.89
  103.3 0.4 copy.32
  103.7 0.4 slice-done
  104.2 0.1 copy.33
  104.2 0.1 iota_compare_fusion.3
  104.3 0.0 copy-done.18
  104.3 0.1 compare_select_fusion
  104.4 0.3 multiply_reduce_fusion.1
  104.8 0.3 copy-done.12
  105.0 0.6 exponential_multiply_fusion
  105.6 1.9 %multiply_add_fusion = f32[2,24,64,128]{3,2,1,0:T(8,128)S(1)} fusion(f32[2,24,64,128]{3,2,1,0:T(8,128)} %param.31, bf16[2,128,24,64]{1,3,2,0:T(8,128)(2,1)S(1)} %bitcast.48, f32[2,128,24]{1,2,0:T(8,128)S(1)} %get-tuple-element.20, f32[2,24]{1,0:T(2,128)S(1)} %exp.41, bf16[2,128,1792]{2,1,0:T(8,128)(2,1)S(1)} %multiply_convert_fusion.1), kind=kOutput, calls=%fused_computation.21 | convolution fusion | flops 102629376 | bytes 4023296 | tf_op jit(solution)/shard_map/gshp,gsn->ghpn/dot_general | solution.py:301
  107.6 0.9 dynamic-slice_convert_fusion
  108.5 0.5 collective-permute-start.2
  109.0 0.8 fusion.33
  109.9 1.3 slice_convert_fusion
  111.2 2.4 %reshape.269 = f32[2,128,24,64]{3,2,1,0:T(8,128)S(1)} reshape(f32[256,1536]{1,0:T(8,128)} %slice_convert_fusion) | data formatting | bytes 3145728 | tf_op jit(solution)/shard_map/reshape | solution.py:271
  113.6 2.0 %copy.36 = f32[2,128,24,64]{1,3,2,0:T(8,128)} copy(f32[2,128,24,64]{3,2,1,0:T(8,128)S(1)} %reshape.269) | data formatting | bytes 3145728 | tf_op jit(solution)/shard_map/reshape | solution.py:271
  115.7 0.8 mul.203
  116.4 0.0 copy-start.22
  116.5 2.7 %fusion.4 = f32[2,24,64,128]{3,2,1,0:T(8,128)S(1)} fusion(bf16[2,128,24,64]{1,3,2,0:T(8,128)(2,1)} %bitcast.49, f32[2,128,24]{1,2,0:T(8,128)} %copy-done.12, f32[2,128,24]{1,2,0:T(8,128)} %copy-done.14, f32[2,128,128]{2,1,0:T(8,128)} %fusion.33, pred[128,128]{1,0:T(8,128)(4,1)S(1)} %iota_compare_fusion.1), kind=kOutput, calls=%fused_computation.15 | convolution fusion | flops 104595456 | bytes 2555904 | tf_op jit(solution)/shard_map/gtsh,gshp->gthp/dot_general | solution.py:261
  119.2 1.8 %multiply_reduce_fusion = (f32[2,128]{1,0:T(2,128)S(1)}, bf16[2,128,24,64]{1,3,2,0:T(8,128)(2,1)S(1)}) fusion(f32[24,64]{1,0:T(8,128)S(1)} %mul.203, f32[2,128,24,64]{1,3,2,0:T(8,128)S(1)} %copy-done.8, bf16[2,128,24,64]{1,3,2,0:T(8,128)(2,1)S(1)} %bitcast.50, f32[24]{0:T(128)S(1)} %copy-done.22, f32[2,24,64,128]{3,2,1,0:T(8,128)S(1)} %copy-done.7, ...), kind=kOutput, calls=%fused_computation.22 | convolution fusion | flops 106561280 | bytes 6388832 | tf_op jit(solution)/shard_map/gtn,ghpn->gthp/dot_general | solution.py:264
  121.0 1.6 %collective-permute-start.1 = (f32[256]{0:T(256)S(1)}, f32[256]{0:T(256)S(1)}, u32[]{:S(2)}, u32[]{:S(2)}) collective-permute-start(f32[256]{0:T(256)S(1)} %bitcast.54), channel_id=1, source_target_pairs={{0,1},{1,0},{2,3},{3,2},{4,5},{5,4},{6,7},{7,6},{8,9},{9,8},{10,11... | collective-permute-start | bytes 3080 | tf_op jit(solution)/shard_map/ppermute | solution.py:185
  122.6 0.8 copy.37
  123.4 3.9 %convolution_convert_fusion.1 = bf16[256,1536]{1,0:T(8,128)(2,1)S(1)} fusion(bf16[1536,1536]{1,0:T(8,128)(2,1)} %bitcast.56, bf16[192,8,2,128]{3,2,1,0:T(2,128)(2,1)S(1)} %bitcast.52), kind=kOutput, calls=%fused_computation.3 | convolution fusion | flops 1208352768 | bytes 6291456 | tf_op jit(solution)/shard_map/dot_general | solution.py:278
  127.4 0.6 collective-permute-start
  128.0 1.2 dynamic_slice.30
  129.2 1.1 compare_convert_fusion.1
  130.3 0.0 collective-permute-done.1
  130.3 0.1 dynamic_slice.29
  130.4 0.0 collective-permute-done.3
  130.4 0.7 fusion.37
  131.2 0.6 pad_maximum_fusion.1
  131.8 0.0 collective-permute-done.2
  131.8 0.2 convert_select_fusion.1
  132.0 1.3 pad_maximum_fusion
  133.3 4.7 %collective-permute-done = bf16[128,1536]{1,0:T(8,128)(2,1)S(1)} collective-permute-done((bf16[128,1536]{1,0:T(8,128)(2,1)S(1)}, bf16[128,1536]{1,0:T(8,128)(2,1)S(1)}, u32[]{:S(2)}, u32[]{:S(2)}) %collective-permute-start) | collective-permute-done | bytes 393248 | tf_op jit(solution)/shard_map/ppermute | solution.py:185
  138.0 1.0 multiply_convert_fusion.4
  (51 shorter events, 0.2 us)
Async XLA Ops:
  96.1 1.2 copy-start.5
  96.1 0.7 copy-start.15
  96.1 0.8 copy-start.17
  97.3 4.6 %copy-start.20 = (s32[2]{0:T(128)S(1)}, s32[2]{0:T(128)}, u32[]{:S(2)}) copy-start(s32[2]{0:T(128)} %param.35) | copy-start | bytes 28
  97.3 4.6 %copy-start.11 = (f32[5,1536]{1,0:T(8,128)S(1)}, f32[5,1536]{1,0:T(8,128)}, u32[]{:S(2)}) copy-start(f32[5,1536]{1,0:T(8,128)} %param.24) | copy-start | bytes 92164
  97.3 4.6 %copy-start.16 = (f32[5,256]{1,0:T(8,128)S(1)}, f32[5,256]{1,0:T(8,128)}, u32[]{:S(2)}) copy-start(f32[5,256]{1,0:T(8,128)} %param.25) | copy-start | bytes 15364
  99.1 0.6 copy-start.9
  99.8 2.3 %copy-start.10 = (bf16[2,3,1536]{2,1,0:T(4,128)(2,1)}, bf16[2,3,1536]{2,1,0:T(4,128)(2,1)S(1)}, u32[]{:S(2)}) copy-start(bf16[2,3,1536]{2,1,0:T(4,128)(2,1)S(1)} %slice.94) | copy-start | bytes 55300
  100.4 30.0 %collective-permute-start.3 = (bf16[1,3,1536]{2,1,0:T(4,128)(2,1)}, bf16[1,3,1536]{2,1,0:T(4,128)(2,1)}, u32[]{:S(2)}, u32[]{:S(2)}) collective-permute-start(bf16[1,3,1536]{2,1,0:T(4,128)(2,1)} %dynamic-slice_convert_fusion.1), channel_id=1, source_target_pairs={{0,1},{1,0},{2,3},{3,2},{4,5},{5,4},{6,7},{7,6},{8,9},{9,8},{10,11... | collective-permute-start | bytes 27656 | tf_op jit(solution)/shard_map/ppermute | solution.py:185
  103.2 5.8 %copy-start.2 = (bf16[2,128,1792]{2,1,0:T(8,128)(2,1)}, bf16[2,128,1792]{2,1,0:T(8,128)(2,1)S(1)}, u32[]{:S(2)}) copy-start(bf16[2,128,1792]{2,1,0:T(8,128)(2,1)S(1)} %multiply_convert_fusion.1) | copy-start | bytes 2752516
  103.2 0.9 slice-start
  103.3 1.0 copy-start.21
  103.3 1.1 copy-start.18
  103.7 3.8 %copy-start.3 = (bf16[2,128,1536]{1,2,0:T(8,128)(2,1)}, bf16[2,128,1536]{1,2,0:T(8,128)(2,1)S(1)}, u32[]{:S(2)}) copy-start(bf16[2,128,1536]{1,2,0:T(8,128)(2,1)S(1)} %copy.32) | copy-start | bytes 2359300
  104.4 0.6 copy-start.12
  104.7 2.9 %copy-start.14 = (f32[2,128,24]{1,2,0:T(8,128)}, f32[2,128,24]{1,2,0:T(8,128)S(1)}, u32[]{:S(2)}) copy-start(f32[2,128,24]{1,2,0:T(8,128)S(1)} %get-tuple-element.25) | copy-start | bytes 73732
  105.6 4.2 %copy-start.6 = (bf16[256,3456]{1,0:T(8,128)(2,1)S(1)}, bf16[256,3456]{1,0:T(8,128)(2,1)}, u32[]{:S(2)}) copy-start(bf16[256,3456]{1,0:T(8,128)(2,1)} %copy-done.5) | copy-start | bytes 5308420
  107.6 2.3 %copy-start = (f32[2,24,64,128]{3,2,1,0:T(8,128)}, f32[2,24,64,128]{3,2,1,0:T(8,128)S(1)}, u32[]{:S(2)}) copy-start(f32[2,24,64,128]{3,2,1,0:T(8,128)S(1)} %multiply_add_fusion) | copy-start | bytes 4718596
  108.5 23.3 %collective-permute-start.2 = (bf16[1,24,64,128]{3,2,1,0:T(8,128)(2,1)}, bf16[1,24,64,128]{3,2,1,0:T(8,128)(2,1)S(1)}, u32[]{:S(2)}, u32[]{:S(2)}) collective-permute-start(bf16[1,24,64,128]{3,2,1,0:T(8,128)(2,1)} %dynamic-slice_convert_fusion), channel_id=1, source_target_pairs={{0,1},{1,0},{2,3},{3,2},{4,5},{5,4},{6,7},{7,6},{8,9},{9,8},{10,11... | collective-permute-start | bytes 1179656 | tf_op jit(solution)/shard_map/ppermute | solution.py:185
  116.4 2.7 %copy-start.4 = (bf16[2,128,1536]{1,2,0:T(8,128)(2,1)S(1)}, bf16[2,128,1536]{1,2,0:T(8,128)(2,1)}, u32[]{:S(2)}) copy-start(bf16[2,128,1536]{1,2,0:T(8,128)(2,1)} %copy-done.3) | copy-start | bytes 2359300
  116.4 2.7 %copy-start.7 = (f32[2,24,64,128]{3,2,1,0:T(8,128)S(1)}, f32[2,24,64,128]{3,2,1,0:T(8,128)}, u32[]{:S(2)}) copy-start(f32[2,24,64,128]{3,2,1,0:T(8,128)} %param.31) | copy-start | bytes 4718596
  116.4 2.7 %copy-start.8 = (f32[2,128,24,64]{1,3,2,0:T(8,128)S(1)}, f32[2,128,24,64]{1,3,2,0:T(8,128)}, u32[]{:S(2)}) copy-start(f32[2,128,24,64]{1,3,2,0:T(8,128)} %copy.36) | copy-start | bytes 4718596
  116.4 2.7 %copy-start.13 = (f32[2,128,24]{1,2,0:T(8,128)S(1)}, f32[2,128,24]{1,2,0:T(8,128)}, u32[]{:S(2)}) copy-start(f32[2,128,24]{1,2,0:T(8,128)} %get-tuple-element.21) | copy-start | bytes 73732
  116.4 2.7 %copy-start.22 = (f32[24]{0:T(128)S(1)}, f32[24]{0:T(128)}, u32[]{:S(2)}) copy-start(f32[24]{0:T(128)} %param.28) | copy-start | bytes 292
  121.0 9.3 %collective-permute-start.1 = (f32[256]{0:T(256)S(1)}, f32[256]{0:T(256)S(1)}, u32[]{:S(2)}, u32[]{:S(2)}) collective-permute-start(f32[256]{0:T(256)S(1)} %bitcast.54), channel_id=1, source_target_pairs={{0,1},{1,0},{2,3},{3,2},{4,5},{5,4},{6,7},{7,6},{8,9},{9,8},{10,11... | collective-permute-start | bytes 3080 | tf_op jit(solution)/shard_map/ppermute | solution.py:185
  123.4 4.5 %slice-start.1 = ((bf16[2,3,1792]{2,1,0:T(4,128)(2,1)}), bf16[2,3,256]{2,1,0:T(4,128)(2,1)S(1)}, s32[]{:S(2)}) async-start(bf16[2,3,1792]{2,1,0:T(4,128)(2,1)} %copy-done.9), calls=%async_computation.1 | async-start | bytes 8192 | tf_op jit(solution)/shard_map/slice | solution.py:345
  123.4 8.4 %copy-start.1 = (f32[2,24,64,128]{3,2,1,0:T(8,128)S(1)}, f32[2,24,64,128]{3,2,1,0:T(8,128)}, u32[]{:S(2)}) copy-start(f32[2,24,64,128]{3,2,1,0:T(8,128)} %copy-done) | copy-start | bytes 4718596
  127.4 10.6 %collective-permute-start = (bf16[128,1536]{1,0:T(8,128)(2,1)S(1)}, bf16[128,1536]{1,0:T(8,128)(2,1)S(1)}, u32[]{:S(2)}, u32[]{:S(2)}) collective-permute-start(bf16[128,1536]{1,0:T(8,128)(2,1)S(1)} %constant_dynamic-slice_fusion), channel_id=1, source_target_pairs={{0,1},{1,0},{2,3},{3,2},{4,5},{5,4},{6,7},{7,6},{8,9},{9,8},{10,11... | collective-permute-start | bytes 1179656 | tf_op jit(solution)/shard_map/ppermute | solution.py:185
  132.0 6.0 %copy-start.19 = (f32[128]{0:T(128)S(1)}, f32[128]{0:T(128)}, u32[]{:S(2)}) copy-start(f32[128]{0:T(128)} %compare_convert_fusion.1) | copy-start | bytes 1540
